TPU v7x, 32 devices: a whole 2x2x4 slice. The times are simulated.
32 devices in a mesh: dp: 8 (over z, y), blk: 4 (over x, core).
Axes of the slice: x: 2, y: 2, z: 4, core: 2. Of those that a mesh axis runs over, the one named last changes fastest.
Arguments:
- token_ids: int32 [8, 128], P('dp'), may hold values from 0 to 50303
- lengths: int32 [8, 16], P('dp'), may hold values from 0 to 128, as said below
- embedding: float32 [50304, 768], P(('dp', 'blk'))
- emb_mean: float32 [50304, 768], P(('dp', 'blk')), may hold values from -9.536743e-07 to 9.536743e-07
- emb_var: float32 [50304, 768], P(('dp', 'blk')), may hold values from 1.1348653e-13 to 1.8332438e-12
- positions: float32 [128, 768], replicated, may hold values from -0.12 to 0.12
- pos_mean: float32 [128, 768], replicated, may hold values from -1.9073486e-06 to 1.9073486e-06
- pos_var: float32 [128, 768], replicated, may hold values from 2.2959198e-13 to 3.6664877e-12
- gains_biases: float32 [14, 768], replicated
- gains_mean: float32 [14, 768], replicated, may hold values from -7.6293945e-06 to 7.6293945e-06
- gains_var: float32 [14, 768], replicated, may hold values from 3.6664877e-12 to 5.8489213e-11
- w_attn: float32 [1, 768, 4, 768], P(None, 'blk', None, 'dp')
- attn_mean: float32 [1, 768, 4, 768], P(None, 'blk', None, 'dp'), may hold values from -1.9073486e-06 to 1.9073486e-06
- attn_var: float32 [1, 768, 4, 768], P(None, 'blk', None, 'dp'), may hold values from 2.2959198e-13 to 3.6664877e-12
- w_fc: float32 [1, 768, 3072], P(None, 'blk', 'dp'), may hold values from -0.21875 to 0.21875
- fc_mean: float32 [1, 768, 3072], P(None, 'blk', 'dp'), may hold values from -1.9073486e-06 to 1.9073486e-06
- fc_var: float32 [1, 768, 3072], P(None, 'blk', 'dp'), may hold values from 2.2959198e-13 to 3.6664877e-12
- w_proj: float32 [1, 3072, 768], P(None, 'blk', 'dp'), may hold values from -0.109375 to 0.109375
- proj_mean: float32 [1, 3072, 768], P(None, 'blk', 'dp'), may hold values from -1.9073486e-06 to 1.9073486e-06
- proj_var: float32 [1, 3072, 768], P(None, 'blk', 'dp'), may hold values from 2.2959198e-13 to 3.6664877e-12
Outputs:
- loss_sum: float32 [], replicated
- token_count: float32 [], replicated
- grad_norm: float32 [], replicated
- emb_grad: float32 [50304, 768], P(('dp', 'blk'))
- emb_var_new: float32 [50304, 768], P(('dp', 'blk'))
- emb_new: float32 [50304, 768], P(('dp', 'blk'))
- pos_grad: float32 [128, 768], replicated
- pos_var_new: float32 [128, 768], replicated
- pos_new: float32 [128, 768], replicated
- gains_grad: float32 [14, 768], replicated
- gains_var_new: float32 [14, 768], replicated
- gains_new: float32 [14, 768], replicated
- attn_grad: float32 [1, 768, 4, 768], P(None, 'blk', None, 'dp')
- attn_var_new: float32 [1, 768, 4, 768], P(None, 'blk', None, 'dp')
- attn_new: float32 [1, 768, 4, 768], P(None, 'blk', None, 'dp')
- fc_grad: float32 [1, 768, 3072], P(None, 'blk', 'dp')
- fc_var_new: float32 [1, 768, 3072], P(None, 'blk', 'dp')
- fc_new: float32 [1, 768, 3072], P(None, 'blk', 'dp')
- proj_grad: float32 [1, 3072, 768], P(None, 'blk', 'dp')
- proj_var_new: float32 [1, 3072, 768], P(None, 'blk', 'dp')
- proj_new: float32 [1, 3072, 768], P(None, 'blk', 'dp')
Inputs may be any that keep to these rules, and one draw needn't show every extreme that they name: Each row holds its packed documents' lengths in order; their sum is the row's live length and the rest of the row is padding. In one row a single document fills all 128 positions.
All inputs are finite; a program needn't handle non-finite values. Where the computation divides by a largest or mean magnitude, that divisor is 1e-20 or more.
Results may differ from a plain program's by a relative error of at most 0.0095.
The roundings to bfloat16 on the way count: a program that leaves them out, or rounds other values in their place, can miss the bound.
Values may be sent and summed in bfloat16 or wider, within the bound.
No kernel may reach another device: no remote copies, remote signals or barrier semaphores. Data moves between devices by JAX's collectives and lax.ppermute only.
A program may use at most 384 MiB of HBM per device.

v0:
```python
import math

import jax
import jax.numpy as jnp
from jax import lax
from jax.sharding import PartitionSpec as P

D = 768
HEADS = 12
HDIM = 64
FF = 3072
LAYERS = 1
STEP = 10


HIGHEST = lax.Precision.HIGHEST
ln_eps = 1e-05
zloss_weight = 0.01
damping = 0.1
clip_level = 0.02
learn_rate = 0.1
beta_first = 0.9
beta_second = 0.95
adam_eps = 1e-08
weight_decay = 0.1


def combined_all(value, axis, join):
    pieces = jax.tree.map(lambda part: lax.all_gather(part, axis), value)
    head = jax.tree.map(lambda part: part[0], pieces)
    tail = jax.tree.map(lambda part: part[1:], pieces)
    running, _ = lax.scan(lambda running, piece: (join(running, piece), None), head, tail)
    return running


def layer_norm(values, gain_vec, shift_vec):
    centered = values - jnp.mean(values, -1, keepdims=True)
    spread = jnp.mean(centered * centered, -1, keepdims=True)
    return centered * lax.rsqrt(spread + ln_eps) * gain_vec + shift_vec


def doc_layout(lengths_row, row_len):
    doc_ends = jnp.cumsum(lengths_row, dtype=jnp.int32)
    spot_index = jnp.arange(row_len, dtype=jnp.int32)
    after_end = doc_ends[None, :] <= spot_index[:, None]
    segment = jnp.sum(after_end.astype(jnp.int32), 1, dtype=jnp.int32)
    start_pos = jnp.sum(jnp.where(after_end, lengths_row[None, :], 0), 1, dtype=jnp.int32)
    local_pos = spot_index - start_pos
    live_len = doc_ends[-1]
    next_seg = jnp.concatenate([segment[1:], jnp.full((1,), -1, jnp.int32)])
    counted = (spot_index + 1 < live_len) & (next_seg == segment)
    attn_mask = (spot_index[None, :] <= spot_index[:, None]) & (
        segment[None, :] == segment[:, None]
    )
    return (local_pos, counted, attn_mask)


def small_rows(gains_biases, layer_index):
    per_layer = 8 + FF // D
    base_row = layer_index * per_layer
    fc_bias = gains_biases[base_row + 7 : base_row + 7 + FF // D].reshape(FF)
    return (
        gains_biases[base_row],
        gains_biases[base_row + 1],
        gains_biases[base_row + 2],
        gains_biases[base_row + 3],
        gains_biases[base_row + 4],
        gains_biases[base_row + 5],
        gains_biases[base_row + 6],
        fc_bias,
        gains_biases[base_row + 7 + FF // D],
    )


def adam_update(weights, mean_old, var_old, gradient, clip_factor, decay):
    clipped = clip_factor * gradient
    new_mean = beta_first * mean_old + (1.0 - beta_first) * clipped
    new_var = beta_second * var_old + (1.0 - beta_second) * clipped * clipped
    mean_hat = new_mean / (1.0 - beta_first**STEP)
    var_hat = new_var / (1.0 - beta_second**STEP)
    updated = weights - learn_rate * (mean_hat / (jnp.sqrt(var_hat) + adam_eps) + decay * weights)
    return (clipped, new_var, updated)


def norm_back(values, gain_vec, shift_vec, cotangent):
    result, pullback = jax.vjp(layer_norm, values, gain_vec, shift_vec)
    return pullback(cotangent)


def gelu_back(hidden, cotangent):
    result, pullback = jax.vjp(lambda inner_val: jax.nn.gelu(inner_val, approximate=True), hidden)
    return pullback(cotangent)[0]


def row_block(values, first_row, row_count):
    return lax.dynamic_slice_in_dim(values, first_row, row_count, values.ndim - 1)


def gram_rows(stacked, first_row, row_count):
    return jnp.einsum(
        "fsi,fsj->fij",
        row_block(stacked, first_row, row_count),
        stacked,
        preferred_element_type=jnp.float32,
    )


def attend(qkv_low, attn_mask):
    seq_len = qkv_low.shape[0]
    head_split = qkv_low.reshape(seq_len, 3, HEADS, HDIM)
    score_scale = 1.0 / math.sqrt(HDIM)
    scores = (
        jnp.einsum(
            "shd,thd->hst", head_split[:, 0], head_split[:, 1], preferred_element_type=jnp.float32
        )
        * score_scale
    )
    attn_probs = jax.nn.softmax(jnp.where(attn_mask[None], scores, -1e30), axis=-1)
    return (head_split, attn_probs, score_scale)


def layer_forward(stream, attn_all, fc_all, proj_all, rows_small, attn_mask):
    gain_one, shift_one, bias_q, bias_v, bias_o, gain_two, shift_two, bias_fc, bias_proj = (
        rows_small
    )
    normed = layer_norm(stream, gain_one, shift_one).astype(jnp.bfloat16)
    qkv_bias = jnp.stack([bias_q, jnp.zeros_like(bias_q), bias_v])
    qkv_low = (
        jnp.einsum("sd,dke->ske", normed, attn_all[:, :3], preferred_element_type=jnp.float32)
        + qkv_bias
    ).astype(jnp.bfloat16)
    head_split, attn_probs, score_scale = attend(qkv_low, attn_mask)
    mixed_out = (
        jnp.einsum(
            "hst,thd->shd",
            attn_probs.astype(jnp.bfloat16),
            head_split[:, 2],
            preferred_element_type=jnp.float32,
        )
        .astype(jnp.bfloat16)
        .reshape(stream.shape)
    )
    middle = (
        stream + jnp.dot(mixed_out, attn_all[:, 3], preferred_element_type=jnp.float32) + bias_o
    )
    normed_two = layer_norm(middle, gain_two, shift_two).astype(jnp.bfloat16)
    hidden = jnp.dot(normed_two, fc_all, preferred_element_type=jnp.float32) + bias_fc
    active = jax.nn.gelu(hidden, approximate=True).astype(jnp.bfloat16)
    result = middle + jnp.dot(active, proj_all, preferred_element_type=jnp.float32) + bias_proj
    return (result, (stream, normed, qkv_low, mixed_out, middle, normed_two, hidden, active))


def layer_backward(
    grad_out,
    saved,
    attn_all,
    fc_all,
    proj_all,
    rows_small,
    attn_mask,
    col_start,
    col_width,
    wide_start,
    wide_width,
):
    stream, normed, qkv_low, mixed_out, middle, normed_two, hidden, active = saved
    gain_one, shift_one, bias_q, bias_v, bias_o, gain_two, shift_two, bias_fc, bias_proj = (
        rows_small
    )
    seq_len, model_width = stream.shape
    grad_proj = grad_out.astype(jnp.bfloat16)
    proj_cols = jnp.einsum(
        "sf,sd->fd",
        active,
        row_block(grad_proj, col_start, col_width),
        preferred_element_type=jnp.float32,
    )
    grad_active = jnp.einsum("sd,fd->sf", grad_proj, proj_all, preferred_element_type=jnp.float32)
    grad_fc = gelu_back(hidden, grad_active).astype(jnp.bfloat16)
    fc_cols = jnp.einsum(
        "sd,sf->df",
        normed_two,
        row_block(grad_fc, wide_start, wide_width),
        preferred_element_type=jnp.float32,
    )
    grad_normed_two = jnp.einsum("sf,df->sd", grad_fc, fc_all, preferred_element_type=jnp.float32)
    back_middle, grad_gain_two, grad_shift_two = norm_back(
        middle, gain_two, shift_two, grad_normed_two
    )
    grad_middle = grad_out + back_middle
    grad_attn_out = grad_middle.astype(jnp.bfloat16)
    out_cols = jnp.einsum(
        "sd,se->de",
        mixed_out,
        row_block(grad_attn_out, col_start, col_width),
        preferred_element_type=jnp.float32,
    )
    grad_mixed = (
        jnp.einsum("se,de->sd", grad_attn_out, attn_all[:, 3], preferred_element_type=jnp.float32)
        .astype(jnp.bfloat16)
        .reshape(seq_len, HEADS, HDIM)
    )
    head_split, attn_probs, score_scale = attend(qkv_low, attn_mask)
    grad_value = jnp.einsum(
        "hst,shd->thd",
        attn_probs.astype(jnp.bfloat16),
        grad_mixed,
        preferred_element_type=jnp.float32,
    )
    grad_probs = jnp.einsum(
        "shd,thd->hst", grad_mixed, head_split[:, 2], preferred_element_type=jnp.float32
    )
    grad_scores = (
        attn_probs * (grad_probs - jnp.sum(grad_probs * attn_probs, -1, keepdims=True))
    ).astype(jnp.bfloat16)
    grad_query = (
        jnp.einsum(
            "hst,thd->shd", grad_scores, head_split[:, 1], preferred_element_type=jnp.float32
        )
        * score_scale
    )
    grad_key = (
        jnp.einsum(
            "hst,shd->thd", grad_scores, head_split[:, 0], preferred_element_type=jnp.float32
        )
        * score_scale
    )
    grad_qkv = (
        jnp.stack([grad_query, grad_key, grad_value], 1)
        .reshape(seq_len, 3, model_width)
        .astype(jnp.bfloat16)
    )
    qkv_cols = jnp.einsum(
        "sd,ske->dke",
        normed,
        row_block(grad_qkv, col_start, col_width),
        preferred_element_type=jnp.float32,
    )
    grad_normed = jnp.einsum(
        "ske,dke->sd", grad_qkv, attn_all[:, :3], preferred_element_type=jnp.float32
    )
    back_stream, grad_gain_one, grad_shift_one = norm_back(stream, gain_one, shift_one, grad_normed)
    grad_stream = grad_middle + back_stream
    col_grads = (jnp.concatenate([qkv_cols, out_cols[:, None]], 1), fc_cols, proj_cols)
    output_grads = jnp.stack(
        [grad_qkv[:, 0], grad_qkv[:, 1], grad_qkv[:, 2], grad_attn_out, grad_proj]
    )
    grad_stats = (
        gram_rows(output_grads, col_start, col_width),
        gram_rows(grad_fc[None], wide_start, wide_width)[0],
    )
    qkv_sums = jnp.sum(grad_qkv.astype(jnp.float32), 0)
    small_grad = jnp.concatenate(
        [
            grad_gain_one[None],
            grad_shift_one[None],
            qkv_sums[0][None],
            qkv_sums[2][None],
            jnp.sum(grad_attn_out.astype(jnp.float32), 0)[None],
            grad_gain_two[None],
            grad_shift_two[None],
            jnp.sum(grad_fc.astype(jnp.float32), 0).reshape(-1, model_width),
            jnp.sum(grad_proj.astype(jnp.float32), 0)[None],
        ],
        0,
    )
    return (grad_stream, col_grads, grad_stats, small_grad)


def sum_inputs(input_small, input_large):
    return lax.psum((input_small, input_large), "dp")


def merge_parts(first_part, second_part):
    top_val = jnp.maximum(first_part[0], second_part[0])
    return (
        top_val,
        first_part[1] * jnp.exp(first_part[0] - top_val)
        + second_part[1] * jnp.exp(second_part[0] - top_val),
        first_part[2] + second_part[2],
    )


def vocab_stats(logits, target_hit):
    local_top = jnp.max(logits, 1)
    local_total = jnp.sum(jnp.exp(logits - local_top[:, None]), 1)
    local_target = jnp.sum(jnp.where(target_hit, logits, 0.0), 1)
    return (local_top, local_total, local_target)


def logit_grads(logits, log_total, target_hit, counted_rows, total_count):
    row_weight = jnp.where(counted_rows, 1.0, 0.0) / total_count
    return (
        row_weight[:, None]
        * (
            (1.0 + 2.0 * zloss_weight * log_total)[:, None] * jnp.exp(logits - log_total[:, None])
            - target_hit.astype(jnp.float32)
        )
    ).astype(jnp.bfloat16)


def start_rows(factor_rows, top_val, first_row):
    row_count, order = (factor_rows.shape[-2], factor_rows.shape[-1])
    eye_rows = (jnp.arange(order)[None, :] == (first_row + jnp.arange(row_count))[:, None]).astype(
        jnp.float32
    )
    shifted = factor_rows / (top_val + 1e-06)[..., None, None] + damping * eye_rows
    kappa_val = 1.0 + damping
    return (
        shifted.astype(jnp.bfloat16),
        2.0 / kappa_val * eye_rows - shifted / (kappa_val * kappa_val),
    )


def newton_step(shifted_low, inverse_rows, full_low):
    product = jnp.einsum(
        "lfij,lfjk->lfik", shifted_low, full_low, preferred_element_type=jnp.float32
    ).astype(jnp.bfloat16)
    return 2.0 * inverse_rows - jnp.einsum(
        "lfij,lfjk->lfik", product, full_low, preferred_element_type=jnp.float32
    )


def body(
    token_ids,
    lengths,
    embedding,
    emb_mean,
    emb_var,
    positions,
    pos_mean,
    pos_var,
    gains_biases,
    gains_mean,
    gains_var,
    w_attn,
    attn_mean,
    attn_var,
    w_fc,
    fc_mean,
    fc_var,
    w_proj,
    proj_mean,
    proj_var,
):
    row_ids = token_ids[0]
    seq_len = row_ids.shape[0]
    model_width = embedding.shape[1]
    dp_size = lax.axis_size("dp")
    blk_size = lax.axis_size("blk")
    dp_index = lax.axis_index("dp")
    blk_index = lax.axis_index("blk")
    local_pos, counted, attn_mask = doc_layout(lengths[0], seq_len)
    targets = jnp.concatenate([row_ids[1:], jnp.zeros((1,), jnp.int32)])
    every_ids, every_lengths = (
        lax.all_gather(token_ids, "dp", axis=0, tiled=True),
        lax.all_gather(lengths, "dp", axis=0, tiled=True),
    )
    every_counted = jax.vmap(lambda lengths_row: doc_layout(lengths_row, seq_len)[1])(every_lengths)
    total_count = jnp.sum(every_counted.astype(jnp.float32))
    tokens = float(seq_len * dp_size)
    attn_all, fc_all, proj_all, table_low = (
        lax.all_gather(w_attn.astype(jnp.bfloat16), "dp", axis=3, tiled=True),
        lax.all_gather(w_fc.astype(jnp.bfloat16), "dp", axis=2, tiled=True),
        lax.all_gather(w_proj.astype(jnp.bfloat16), "dp", axis=2, tiled=True),
        lax.all_gather(embedding.astype(jnp.bfloat16), "dp", axis=0, tiled=True),
    )
    attn_all, fc_all, proj_all = (
        lax.all_gather(attn_all, "blk", axis=1, tiled=True),
        lax.all_gather(fc_all, "blk", axis=1, tiled=True),
        lax.all_gather(proj_all, "blk", axis=1, tiled=True),
    )
    piece_rows = embedding.shape[0]
    group_rows = piece_rows * blk_size
    in_mine = row_ids % group_rows // piece_rows == blk_index
    in_slot = row_ids // group_rows * piece_rows + row_ids % piece_rows
    target_mine = targets % group_rows // piece_rows == blk_index
    target_slot = targets // group_rows * piece_rows + targets % piece_rows
    picked = jnp.where(in_mine[:, None], table_low[in_slot].astype(jnp.float32), 0.0)
    embedded = lax.psum(picked.astype(jnp.bfloat16), "blk").astype(jnp.float32)
    pos_onehot = (local_pos[:, None] == jnp.arange(seq_len, dtype=jnp.int32)[None, :]).astype(
        jnp.float32
    )
    stream = embedded + jnp.dot(pos_onehot, positions, precision=HIGHEST)
    col_width = model_width // blk_size
    col_start = blk_index * col_width
    wide_width = fc_all.shape[2] // blk_size
    wide_start = blk_index * wide_width
    input_small = []
    input_large = []
    layer_index = 0
    stream, saved = layer_forward(
        stream,
        attn_all[layer_index],
        fc_all[layer_index],
        proj_all[layer_index],
        small_rows(gains_biases, layer_index),
        attn_mask,
    )
    saved_all = [saved]
    input_small.append(gram_rows(jnp.stack([saved[1], saved[3], saved[5]]), col_start, col_width))
    input_large.append(gram_rows(saved[7][None], wide_start, wide_width)[0])
    input_small = jnp.stack(input_small)
    input_large = jnp.stack(input_large)
    final_row = LAYERS * (8 + FF // D)
    final_low = layer_norm(stream, gains_biases[final_row], gains_biases[final_row + 1]).astype(
        jnp.bfloat16
    )
    logits = jnp.einsum("sd,vd->sv", final_low, table_low, preferred_element_type=jnp.float32)
    slot_cols = jnp.arange(logits.shape[1], dtype=jnp.int32)
    target_hit = target_mine[:, None] & (slot_cols[None, :] == target_slot[:, None])
    top_all, total_all, target_logit = combined_all(
        vocab_stats(logits, target_hit), "blk", merge_parts
    )
    mine_total = top_all + jnp.log(total_all)
    grad_logits = logit_grads(logits, mine_total, target_hit, counted, total_count)
    head_partial = jnp.dot(grad_logits, table_low, preferred_element_type=jnp.float32)
    loss_local = jnp.sum(
        jnp.where(counted, mine_total - target_logit + zloss_weight * mine_total * mine_total, 0.0)
    )
    grad_final = lax.psum(head_partial, "blk")
    grad_stream, grad_gain_final, grad_shift_final = norm_back(
        stream, gains_biases[final_row], gains_biases[final_row + 1], grad_final
    )
    col_list = [None] * LAYERS
    stat_list = [None] * LAYERS
    small_list = [None] * LAYERS
    for layer_index in reversed(range(LAYERS)):
        grad_stream, col_grads, grad_stats, small_grad = layer_backward(
            grad_stream,
            saved_all[layer_index],
            attn_all[layer_index],
            fc_all[layer_index],
            proj_all[layer_index],
            small_rows(gains_biases, layer_index),
            attn_mask,
            col_start,
            col_width,
            wide_start,
            wide_width,
        )
        col_list[layer_index] = col_grads
        stat_list[layer_index] = grad_stats
        small_list[layer_index] = small_grad
    grad_embed = grad_stream.astype(jnp.bfloat16)
    local_pos_grad = jnp.dot(pos_onehot.T, grad_stream, precision=HIGHEST)
    right_side = jnp.concatenate([final_low, grad_embed], 0)
    slots = jnp.arange(piece_rows * lax.axis_size("dp"), dtype=jnp.int32)
    left_side = jnp.concatenate(
        [
            grad_logits,
            (in_mine[:, None] & (in_slot[:, None] == slots[None, :])).astype(jnp.bfloat16),
        ],
        0,
    )
    grad_table = lax.psum_scatter(
        jnp.einsum("sv,sd->vd", left_side, right_side, preferred_element_type=jnp.float32),
        "dp",
        scatter_dimension=0,
        tiled=True,
    )
    input_small, input_large = sum_inputs(input_small, input_large)
    small_local = jnp.concatenate(small_list + [grad_gain_final[None], grad_shift_final[None]], 0)
    sum_attn, sum_fc, sum_proj, output_small, output_large, grad_small, grad_pos, loss_sum = (
        lax.psum(
            (
                jnp.stack([item[0] for item in col_list]),
                jnp.stack([item[1] for item in col_list]),
                jnp.stack([item[2] for item in col_list]),
                jnp.stack([item[0] for item in stat_list]),
                jnp.stack([item[1] for item in stat_list]),
                small_local,
                local_pos_grad,
                loss_local,
            ),
            "dp",
        )
    )
    grad_scale = total_count * total_count / tokens
    small_factors = jnp.concatenate([input_small / tokens, output_small * grad_scale], 1)
    large_factors = jnp.stack([input_large / tokens, output_large * grad_scale], 1)
    small_top, large_top = lax.pmax(
        (
            jnp.max(jnp.sum(jnp.abs(small_factors), -1), -1),
            jnp.max(jnp.sum(jnp.abs(large_factors), -1), -1),
        ),
        "blk",
    )
    shifted_small, inverse_small = start_rows(small_factors, small_top, col_start)
    shifted_large, inverse_large = start_rows(large_factors, large_top, wide_start)
    full_small = lax.all_gather(inverse_small.astype(jnp.bfloat16), "blk", axis=2, tiled=True)
    full_large = lax.all_gather(inverse_large.astype(jnp.bfloat16), "blk", axis=2, tiled=True)
    inverse_small = newton_step(shifted_small, inverse_small, full_small)
    inverse_large = newton_step(shifted_large, inverse_large, full_large)
    narrow_cols = model_width // dp_size
    narrow_start = dp_index * narrow_cols
    wide_cols = fc_all.shape[2] // dp_size
    wide_first = dp_index * wide_cols
    right_attn = lax.dynamic_slice_in_dim(inverse_small[:, 3:7], narrow_start, narrow_cols, 3)
    right_proj = lax.dynamic_slice_in_dim(inverse_small[:, 7], narrow_start, narrow_cols, 2)
    right_fc = lax.dynamic_slice_in_dim(inverse_large[:, 1], wide_first, wide_cols, 2)
    mid_attn, mid_fc, mid_proj = lax.psum(
        (
            jnp.einsum("ldmk,lmkc->ldmc", sum_attn, right_attn, precision=HIGHEST),
            jnp.einsum("ldk,lkc->ldc", sum_fc, right_fc, precision=HIGHEST),
            jnp.einsum("lfk,lkc->lfc", sum_proj, right_proj, precision=HIGHEST),
        ),
        "blk",
    )
    left_attn = jnp.stack(
        [inverse_small[:, 0], inverse_small[:, 0], inverse_small[:, 0], inverse_small[:, 1]], 1
    )
    pre_attn = jnp.einsum("lmrd,ldmc->lrmc", left_attn, mid_attn, precision=HIGHEST)
    pre_fc = jnp.einsum("lrd,ldc->lrc", inverse_small[:, 2], mid_fc, precision=HIGHEST)
    pre_proj = jnp.einsum("lrf,lfc->lrc", inverse_large[:, 0], mid_proj, precision=HIGHEST)
    local_squares = (
        jnp.sum(pre_attn * pre_attn)
        + jnp.sum(pre_fc * pre_fc)
        + jnp.sum(pre_proj * pre_proj)
        + jnp.sum(grad_table * grad_table)
    )
    squares = (
        lax.psum(local_squares, ("dp", "blk"))
        + jnp.sum(grad_small * grad_small)
        + jnp.sum(grad_pos * grad_pos)
    )
    grad_norm = jnp.sqrt(squares)
    clip_factor = clip_level / jnp.maximum(grad_norm, clip_level)
    emb_out = adam_update(embedding, emb_mean, emb_var, grad_table, clip_factor, weight_decay)
    pos_out = adam_update(positions, pos_mean, pos_var, grad_pos, clip_factor, weight_decay)
    gains_out = adam_update(gains_biases, gains_mean, gains_var, grad_small, clip_factor, 0.0)
    attn_out = adam_update(w_attn, attn_mean, attn_var, pre_attn, clip_factor, weight_decay)
    fc_out = adam_update(w_fc, fc_mean, fc_var, pre_fc, clip_factor, weight_decay)
    proj_out = adam_update(w_proj, proj_mean, proj_var, pre_proj, clip_factor, weight_decay)
    return (
        loss_sum,
        total_count,
        grad_norm,
        emb_out[0],
        emb_out[1],
        emb_out[2],
        pos_out[0],
        pos_out[1],
        pos_out[2],
        gains_out[0],
        gains_out[1],
        gains_out[2],
        attn_out[0],
        attn_out[1],
        attn_out[2],
        fc_out[0],
        fc_out[1],
        fc_out[2],
        proj_out[0],
        proj_out[1],
        proj_out[2],
    )


def solution(mesh):
    return jax.shard_map(
        body,
        mesh=mesh,
        in_specs=(
            P("dp", None),
            P("dp", None),
            P(("dp", "blk"), None),
            P(("dp", "blk"), None),
            P(("dp", "blk"), None),
            P(),
            P(),
            P(),
            P(),
            P(),
            P(),
            P(None, "blk", None, "dp"),
            P(None, "blk", None, "dp"),
            P(None, "blk", None, "dp"),
            P(None, "blk", "dp"),
            P(None, "blk", "dp"),
            P(None, "blk", "dp"),
            P(None, "blk", "dp"),
            P(None, "blk", "dp"),
            P(None, "blk", "dp"),
        ),
        out_specs=(
            P(),
            P(),
            P(),
            P(("dp", "blk"), None),
            P(("dp", "blk"), None),
            P(("dp", "blk"), None),
            P(),
            P(),
            P(),
            P(),
            P(),
            P(),
            P(None, "blk", None, "dp"),
            P(None, "blk", None, "dp"),
            P(None, "blk", None, "dp"),
            P(None, "blk", "dp"),
            P(None, "blk", "dp"),
            P(None, "blk", "dp"),
            P(None, "blk", "dp"),
            P(None, "blk", "dp"),
            P(None, "blk", "dp"),
        ),
        check_vma=False,
    )
```

profile of v0, /device:TPU:1, one launch (start us, length us, event | category | flops | bytes accessed | tf_op | source)
XLA Modules:
  0.0 3065.1 jit_solution(445742005024137977)
XLA Ops:
  7.3 4.1 convert_bitcast_fusion
  14.1 371.3 %all-gather.34.cloned.1.call-done = bf16[8,1572,768]{2,1,0:T(8,128)(2,1)} async-done(((bf16[1,1572,768]{2,1,0:T(8,128)(2,1)}), bf16[8,1572,768]{2,1,0:T(8,128)(2,1)}) %all-gather.34.cloned.1.call-update) | async-done | bytes 19316752 | tf_op jit(solution)/shard_map/all_gather | solution.py:366
  385.3 22.1 reshape.904
  407.4 10.0 gather_fusion
  418.3 13.4 all-gather.18.cloned.1.call-done
  435.3 37.0 %all-gather.22.cloned.1.call-done = bf16[1,192,3072]{2,1,0:T(8,128)(2,1)} async-done(((bf16[1,192,384]{2,1,0:T(8,128)(2,1)}), bf16[1,192,3072]{2,1,0:T(8,128)(2,1)}) %all-gather.22.cloned.1.call-update) | async-done | bytes 1179664 | tf_op jit(solution)/shard_map/all_gather | solution.py:364
  472.3 43.6 %all-gather.26.cloned.1.call-done = bf16[1,768,768]{1,2,0:T(8,128)(2,1)} async-done(((bf16[1,768,96]{1,2,0:T(8,128)(2,1)}), bf16[1,768,768]{1,2,0:T(8,128)(2,1)}) %all-gather.26.cloned.1.call-update) | async-done | bytes 1179664 | tf_op jit(solution)/shard_map/all_gather | solution.py:365
  516.8 14.7 all-gather.7
  534.9 14.2 all-reduce.12.cloned.1.call-done
  550.7 39.8 %all-gather.20.cloned.1.call-done = bf16[1,768,4,768]{3,1,2,0:T(8,128)(2,1)} async-done(((bf16[1,192,4,768]{3,1,2,0:T(8,128)(2,1)}), bf16[1,768,4,768]{3,1,2,0:T(8,128)(2,1)}) %all-gather.20.cloned.1.call-update) | async-done | bytes 4718608 | tf_op jit(solution)/shard_map/all_gather | solution.py:369
  597.4 32.3 %all-gather.24.cloned.1.call-done = bf16[1,768,3072]{2,1,0:T(8,128)(2,1)} async-done(((bf16[1,192,3072]{2,1,0:T(8,128)(2,1)}), bf16[1,768,3072]{2,1,0:T(8,128)(2,1)}) %all-gather.24.cloned.1.call-update) | async-done | bytes 4718608 | tf_op jit(solution)/shard_map/all_gather | solution.py:370
  629.6 4.8 multiply_convert_fusion.1
  634.4 34.4 %all-gather.28.cloned.1.call-done = bf16[1,3072,768]{1,2,0:T(8,128)(2,1)} async-done(((bf16[1,768,768]{1,2,0:T(8,128)(2,1)}), bf16[1,3072,768]{1,2,0:T(8,128)(2,1)}) %all-gather.28.cloned.1.call-update) | async-done | bytes 4718608 | tf_op jit(solution)/shard_map/all_gather | solution.py:371
  673.9 9.3 fusion.201
  683.2 5.1 all-gather.4
  690.6 5.0 all-gather.5
  695.6 5.0 all-gather.6
  702.4 4.4 multiply_convert_fusion
  706.9 8.8 fusion.202
  720.1 6.3 convolution_bitcast_fusion.1
  726.4 20.0 all-reduce.14.cloned.1.call-done
  750.6 5.5 convert_reduce_fusion
  774.3 4.7 multiply_reduce_fusion.5
  781.1 5.1 convolution_bitcast_fusion
  801.7 4.2 convolution_bitcast_fusion.2
  811.5 921.2 %all-reduce.16.cloned.1.call-done = (f32[768,4,192]{0,2,1:T(8,128)}, f32[1,5,192,768]{3,2,1,0:T(8,128)}, f32[1,3,192,768]{3,2,1,0:T(8,128)}, f32[768,768]{1,0:T(...) async-done(((f32[768,4,192]{0,2,1:T(8,128)}, f32[1,5,192,768]{3,2,1,0:T(8,128)}, ...) | async-done | bytes 31064080 | tf_op jit(solution)/shard_map/psum | solution.py:465
  1738.6 15.8 broadcast_multiply_fusion.1
  1754.4 7.8 abs_reduce_fusion
  1762.4 5.7 all-reduce.6
  1768.0 4.8 subtract_convert_fusion.1
  1773.0 10.6 fusion.22
  1783.7 16.2 subtract_convert_fusion
  1811.4 18.3 fusion.23
  1830.0 14.6 fusion.242
  1844.6 20.0 subtract_bitcast_fusion.1
  1868.4 4.5 convolution_bitcast_fusion.4
  1875.5 190.9 %all-gather.32.cloned.1.call-done = bf16[1,2,3072,3072]{3,2,1,0:T(8,128)(2,1)} async-done(((bf16[1,2,768,3072]{3,2,1,0:T(8,128)(2,1)}), bf16[1,2,3072,3072]{3,2,1,0:T(8,128)(2,1)}) %all-gather.32.cloned.1.call-update) | async-done | bytes 37748752 | tf_op jit(solution)/shard_map/all_gather | solution.py:492
  2066.4 37.0 %fusion.11 = bf16[2,768,3072]{2,1,0:T(8,128)(2,1)} fusion(bf16[1,2,3072,3072]{3,2,1,0:T(8,128)(2,1)} %all-gather.32.cloned.1.call-done, bf16[2,768,3072]{2,1,0:T(8,128)(2,1)} %fusion.242), kind=kOutput, calls=%fused_computation.14 | convolution fusion | flops 28991029248 | bytes 56623104 | tf_op jit(solution)/shard_map/lfij,lfjk->lfik/dot_general | solution.py:316
  2103.4 37.6 %fusion.9 = f32[2,768,3072]{2,1,0:T(8,128)} fusion(bf16[1,2,3072,3072]{3,2,1,0:T(8,128)(2,1)} %all-gather.32.cloned.1.call-done, bf16[2,768,3072]{2,1,0:T(8,128)(2,1)} %fusion.11), kind=kOutput, calls=%fused_computation.12 | convolution fusion | flops 28991029248 | bytes 66060288 | tf_op jit(solution)/shard_map/lfij,lfjk->lfik/dot_general | solution.py:319
  2141.0 23.4 subtract_bitcast_fusion
  2168.8 4.9 fusion.101
  2173.8 742.4 %fusion = f32[1576,768]{1,0:T(8,128)} fusion(f32[12576,768]{1,0:T(8,128)} %fusion.23), kind=kCustom, calls=%all-reduce-scatter | all-reduce-scatter fusion | flops 9682945 | bytes 43475456
  2918.8 28.8 all-reduce.3
  2948.2 13.3 concatenate.102
  2961.6 4.2 multiply_reduce_fusion
  2969.1 12.1 multiply_reduce_fusion.13
  2988.2 44.1 %psum.125 = f32[]{:T(128)} all-reduce(f32[]{:T(128)S(6)} %add.555), channel_id=1, replica_groups=mesh['dp'=8,'blk'=4] {'dp','blk'}, use_global_device_ids=true, to_apply=%region_51.52 | all-reduce | flops 1 | bytes 8 | tf_op jit(solution)/shard_map/psum | solution.py:523
  3040.1 13.2 multiply_subtract_fusion
  (351 shorter events, 125.6 us)
Async XLA Ops:
  7.2 378.1 %all-gather.34.cloned.1.call-start = ((), (), s32[]{:S(2)}) async-start(), calls=%async_computation.10 | async-start | bytes 21786624 | tf_op jit(solution)/shard_map/all_gather | solution.py:366
  11.4 420.2 %all-gather.18.cloned.1.call-start = ((), (), s32[]{:S(2)}) async-start(), calls=%async_computation.1 | async-start | bytes 1769472 | tf_op jit(solution)/shard_map/all_gather | solution.py:363
  12.4 459.9 %all-gather.22.cloned.1.call-start = ((), (), s32[]{:S(2)}) async-start(), calls=%async_computation.3 | async-start | bytes 1327104 | tf_op jit(solution)/shard_map/all_gather | solution.py:364
  13.2 502.8 %all-gather.26.cloned.1.call-start = ((), (), s32[]{:S(2)}) async-start(), calls=%async_computation.5 | async-start | bytes 1327104 | tf_op jit(solution)/shard_map/all_gather | solution.py:365
  13.9 535.2 %all-reduce.12.cloned.1.call-start = ((), (), s32[]{:S(2)}) async-start(), calls=%async_computation | async-start | bytes 393216 | tf_op jit(solution)/shard_map/psum | solution.py:380
  407.4 108.7 %copy-start.66 = (s32[1,16]{1,0:T(1,128)S(1)}, s32[1,16]{1,0:T(1,128)}, u32[]{:S(2)}) copy-start(s32[1,16]{1,0:T(1,128)} %param.23) | copy-start | bytes 196
  407.4 124.7 %copy-start.54 = (f32[14,768]{1,0:T(8,128)S(1)}, f32[14,768]{1,0:T(8,128)}, u32[]{:S(2)}) copy-start(f32[14,768]{1,0:T(8,128)} %param.30) | copy-start | bytes 129028
  407.4 141.7 %copy-start.35 = (f32[128,768]{1,0:T(8,128)S(1)}, f32[128,768]{1,0:T(8,128)}, u32[]{:S(2)}) copy-start(f32[128,768]{1,0:T(8,128)} %param.27) | copy-start | bytes 1179652
  418.2 172.3 %all-gather.20.cloned.1.call-start = ((), (), s32[]{:S(2)}) async-start(), calls=%async_computation.2 | async-start | bytes 5898240 | tf_op jit(solution)/shard_map/all_gather | solution.py:369
  435.2 194.4 %all-gather.24.cloned.1.call-start = ((), (), s32[]{:S(2)}) async-start(), calls=%async_computation.4 | async-start | bytes 5898240 | tf_op jit(solution)/shard_map/all_gather | solution.py:370
  472.3 196.5 %all-gather.28.cloned.1.call-start = ((), (), s32[]{:S(2)}) async-start(), calls=%async_computation.6 | async-start | bytes 5898240 | tf_op jit(solution)/shard_map/all_gather | solution.py:371
  516.0 230.4 %all-reduce.14.cloned.1.call-start = ((), (), s32[]{:S(2)}) async-start(), calls=%async_computation.7 | async-start | bytes 786432 | tf_op jit(solution)/shard_map/psum | solution.py:421
  550.5 151.0 %copy-start.6 = (f32[128,768]{1,0:T(8,128)}, f32[128,768]{1,0:T(8,128)S(1)}, u32[]{:S(2)}) copy-start(f32[128,768]{1,0:T(8,128)S(1)} %get-tuple-element.249) | copy-start | bytes 1179652
  593.5 36.1 %copy-start.30 = (bf16[128,3,768]{0,2,1:T(8,128)(2,1)}, bf16[128,3,768]{0,2,1:T(8,128)(2,1)S(1)}, u32[]{:S(2)}) copy-start(bf16[128,3,768]{0,2,1:T(8,128)(2,1)S(1)} %copy.120) | copy-start | bytes 1769476
  597.2 103.5 %copy-start.2 = (f32[128,768]{1,0:T(8,128)}, f32[128,768]{1,0:T(8,128)S(1)}, u32[]{:S(2)}) copy-start(f32[128,768]{1,0:T(8,128)S(1)} %get-tuple-element.253) | copy-start | bytes 1179652
  634.4 48.7 %copy-start.13 = (bf16[128,3072]{1,0:T(8,128)(2,1)}, bf16[128,3072]{1,0:T(8,128)(2,1)S(1)}, u32[]{:S(2)}) copy-start(bf16[128,3072]{1,0:T(8,128)(2,1)S(1)} %get-tuple-element.254) | copy-start | bytes 2359300
  715.7 1017.0 %all-reduce.16.cloned.1.call-start = ((), (), s32[]{:S(2)}) async-start(), calls=%async_computation.11 | async-start | bytes 62128128 | tf_op jit(solution)/shard_map/psum | solution.py:465
  809.0 1035.6 %all-gather.30.cloned.1.call-start = ((), (), s32[]{:S(2)}) async-start(), calls=%async_computation.8 | async-start | bytes 11796480 | tf_op jit(solution)/shard_map/all_gather | solution.py:491
  1772.9 293.5 %all-gather.32.cloned.1.call-start = ((), (), s32[]{:S(2)}) async-start(), calls=%async_computation.9 | async-start | bytes 47185920 | tf_op jit(solution)/shard_map/all_gather | solution.py:492
  1799.9 1165.9 %all-reduce.18.cloned.1.call-start = ((), (), s32[]{:S(2)}) async-start(), calls=%async_computation.12 | async-start | bytes 7077888 | tf_op jit(solution)/shard_map/psum | solution.py:502
  1811.4 18.3 copy-start.10
  1830.0 14.7 copy-start.21
  2066.4 74.6 %slice-start.3 = ((s8[9437184]{0:T(1024)(128)(4,1)}), s8[4194304]{0:T(1024)(128)(4,1)S(1)}, s32[]{:S(2)}) async-start(s8[9437184]{0:T(1024)(128)(4,1)} %bitcast.353), calls=%async_computation.16 | async-start | bytes 8388608
  2066.4 74.6 %slice-start.4 = ((s8[9437184]{0:T(1024)(128)(4,1)}), s8[4194304]{0:T(1024)(128)(4,1)S(1)}, s32[]{:S(2)}) async-start(s8[9437184]{0:T(1024)(128)(4,1)} %bitcast.353), calls=%async_computation.17 | async-start | bytes 8388608
  2103.4 37.6 %slice-start.5 = ((s8[9437184]{0:T(1024)(128)(4,1)}), s8[1048576]{0:T(1024)(128)(4,1)S(1)}, s32[]{:S(2)}) async-start(s8[9437184]{0:T(1024)(128)(4,1)} %bitcast.353), calls=%async_computation.18 | async-start | bytes 2097152
  2173.7 742.5 %copy-start.68 = (f32[768]{0:T(1024)S(1)}, f32[768]{0:T(1024)}, u32[]{:S(2)}) copy-start(f32[768]{0:T(1024)} %get-tuple-element.153) | copy-start | bytes 9220
  2173.7 742.5 %copy-start.67 = (f32[768]{0:T(1024)S(1)}, f32[768]{0:T(1024)}, u32[]{:S(2)}) copy-start(f32[768]{0:T(1024)} %get-tuple-element.157) | copy-start | bytes 9220
  2173.7 742.5 %copy-start.64 = (f32[768]{0:T(1024)S(1)}, f32[768]{0:T(1024)}, u32[]{:S(2)}) copy-start(f32[768]{0:T(1024)} %get-tuple-element.220) | copy-start | bytes 9220
  2173.7 742.5 %copy-start.63 = (f32[768]{0:T(1024)S(1)}, f32[768]{0:T(1024)}, u32[]{:S(2)}) copy-start(f32[768]{0:T(1024)} %get-tuple-element.151) | copy-start | bytes 9220
  2173.8 742.5 %copy-start.62 = (f32[768]{0:T(1024)S(1)}, f32[768]{0:T(1024)}, u32[]{:S(2)}) copy-start(f32[768]{0:T(1024)} %get-tuple-element.156) | copy-start | bytes 9220
  2173.8 742.5 %copy-start.65 = (f32[3072]{0:T(1024)S(1)}, f32[3072]{0:T(1024)}, u32[]{:S(2)}) copy-start(f32[3072]{0:T(1024)} %get-tuple-element.264) | copy-start | bytes 36868
  2173.8 742.5 %copy-start.61 = (f32[768]{0:T(1024)S(1)}, f32[768]{0:T(1024)}, u32[]{:S(2)}) copy-start(f32[768]{0:T(1024)} %get-tuple-element.218) | copy-start | bytes 9220
  2173.8 742.6 %copy-start.60 = (f32[768]{0:T(1024)S(1)}, f32[768]{0:T(1024)}, u32[]{:S(2)}) copy-start(f32[768]{0:T(1024)} %get-tuple-element.149) | copy-start | bytes 9220
  2173.8 742.6 %copy-start.59 = (f32[768]{0:T(1024)S(1)}, f32[768]{0:T(1024)}, u32[]{:S(2)}) copy-start(f32[768]{0:T(1024)} %get-tuple-element.155) | copy-start | bytes 9220
  2173.8 743.5 %copy-start.58 = (f32[3,768]{1,0:T(4,128)S(1)}, f32[3,768]{1,0:T(4,128)}, u32[]{:S(2)}) copy-start(f32[3,768]{1,0:T(4,128)} %get-tuple-element.223) | copy-start | bytes 27652
  2917.5 30.7 %collective-permute-start = (f32[28,768]{1,0:T(8,128)S(1)}, f32[28,768]{1,0:T(8,128)S(1)}, u32[]{:S(2)}, u32[]{:S(2)}) collective-permute-start(f32[28,768]{1,0:T(8,128)S(1)} %slice.197), channel_id=1, source_target_pairs={{0,4},{4,8},{8,12},{12,16},{16,20},{20,24},{24,28},{1,5},{5,9},{9,... | collective-permute-start | bytes 258056
  2947.6 14.0 copy-start.52
  2969.0 18.5 copy-start.37
  2969.0 65.3 %copy-start.19 = (f32[1,192,4,96]{1,3,2,0:T(8,128)S(1)}, f32[1,192,4,96]{1,3,2,0:T(8,128)}, u32[]{:S(2)}) copy-start(f32[1,192,4,96]{1,3,2,0:T(8,128)} %copy.134) | copy-start | bytes 884740
  2969.0 65.3 %copy-start.33 = (f32[1,192,4,96]{1,3,2,0:T(8,128)S(1)}, f32[1,192,4,96]{1,3,2,0:T(8,128)}, u32[]{:S(2)}) copy-start(f32[1,192,4,96]{1,3,2,0:T(8,128)} %copy.137) | copy-start | bytes 884740
  2969.0 65.3 %copy-start.34 = (f32[1,192,4,96]{1,3,2,0:T(8,128)S(1)}, f32[1,192,4,96]{1,3,2,0:T(8,128)}, u32[]{:S(2)}) copy-start(f32[1,192,4,96]{1,3,2,0:T(8,128)} %copy.135) | copy-start | bytes 884740
  3040.0 14.5 copy-start.53
  3040.0 14.4 copy-start.55
  3040.0 14.4 copy-start.56
  3040.0 14.4 copy-start.57
  3040.0 15.1 copy-start.39
  3040.1 15.1 copy-start.48
  3040.1 15.1 copy-start.49
  (49 other events, 321.8 us)
Sparse Core Ops, SparseCore 0:
  11.5 373.7 all-gather.33
  388.1 43.5 all-gather.17
  434.3 37.9 all-gather.21
  474.9 41.0 all-gather.25
  518.7 30.3 all-reduce.11
  551.2 39.2 all-gather.19
  592.1 37.4 all-gather.23
  631.3 37.5 all-gather.27
  715.8 30.5 all-reduce.13
  809.1 923.5 all-reduce.15
  1773.0 63.9 all-gather.29
  1838.4 227.8 all-gather.31
  2173.8 74.6 all-reduce.17
where the time goes:
time: 3070 us
  waiting for transfers between devices  1720 us (56%)
  blocking collectives  851 us (28%)
  matrix products  226 us (7%)
  other arithmetic  158 us (5%)
  local copies, waits for them, and re-layouts  86.8 us (3%)
    psum x1, waiting for transfers between devices, body(): lax.psum((jnp.stack([item[0] for item in col_list]), jnp.stack([item[1] f...  921 us
    unnamed x1, blocking collectives  742 us
    all_gather x1, waiting for transfers between devices, body(): lax.all_gather(embedding.astype(jnp.bfloat16), 'dp', axis=0, tiled=True)  371 us
    all_gather x1, waiting for transfers between devices, body(): lax.all_gather(inverse_large.astype(jnp.bfloat16), 'blk', axis=2, tiled=T...  191 us
  transfers between devices with their start and end apart: 14, of which 11 were waited for; matrix products, arithmetic and copies ran while one was open for 30% of the time, Pallas kernels for 0%

commit v1 on v0

v1 whole, which is shorter than its diff:
```python
import math

import jax
import jax.numpy as jnp
from jax import lax
from jax.sharding import PartitionSpec as P

D = 768
HEADS = 12
HDIM = 64
FF = 3072
STEP = 10

HIGHEST = lax.Precision.HIGHEST
ln_eps = 1e-05
zloss_weight = 0.01
damping = 0.1
clip_level = 0.02
learn_rate = 0.1
beta_first = 0.9
beta_second = 0.95
adam_eps = 1e-08
weight_decay = 0.1
kappa = 1.0 + damping
bf16 = jnp.bfloat16
f32 = jnp.float32


def dot(spec, left, right):
    return jnp.einsum(spec, left, right, preferred_element_type=f32)


def xor_permute(value, axis, bit):
    size = lax.axis_size(axis)
    return lax.ppermute(value, axis, [(k, k ^ bit) for k in range(size)])


def spread(value, axes):
    count = 1
    for name in axes if isinstance(axes, tuple) else (axes,):
        count *= lax.axis_size(name)
    copies = jnp.broadcast_to(value[None], (count,) + value.shape)
    return lax.all_to_all(copies, axes, split_axis=0, concat_axis=0)


def by_order(bit, mine, other, axis):
    first = jnp.where(bit == 0, mine, other)
    second = jnp.where(bit == 0, other, mine)
    return jnp.stack([first, second], axis)


def layer_norm(values, gain_vec, shift_vec):
    centered = values - jnp.mean(values, -1, keepdims=True)
    spread_val = jnp.mean(centered * centered, -1, keepdims=True)
    return centered * lax.rsqrt(spread_val + ln_eps) * gain_vec + shift_vec


def norm_back(values, gain_vec, cotangent):
    centered = values - jnp.mean(values, -1, keepdims=True)
    rstd = lax.rsqrt(jnp.mean(centered * centered, -1, keepdims=True) + ln_eps)
    unit = centered * rstd
    scaled = cotangent * gain_vec
    result = rstd * (
        scaled
        - jnp.mean(scaled, -1, keepdims=True)
        - unit * jnp.mean(scaled * unit, -1, keepdims=True)
    )
    return result, jnp.sum(cotangent * unit, 0), jnp.sum(cotangent, 0)


def doc_layout(lengths_row, row_len):
    doc_ends = jnp.cumsum(lengths_row, dtype=jnp.int32)
    spot_index = jnp.arange(row_len, dtype=jnp.int32)
    after_end = doc_ends[None, :] <= spot_index[:, None]
    segment = jnp.sum(after_end.astype(jnp.int32), 1, dtype=jnp.int32)
    start_pos = jnp.sum(jnp.where(after_end, lengths_row[None, :], 0), 1, dtype=jnp.int32)
    local_pos = spot_index - start_pos
    live_len = doc_ends[-1]
    next_seg = jnp.concatenate([segment[1:], jnp.full((1,), -1, jnp.int32)])
    counted = (spot_index + 1 < live_len) & (next_seg == segment)
    attn_mask = (spot_index[None, :] <= spot_index[:, None]) & (
        segment[None, :] == segment[:, None]
    )
    return (local_pos, counted, attn_mask)


def adam_update(weights, mean_old, var_old, gradient, clip_factor, decay):
    clipped = clip_factor * gradient
    new_mean = beta_first * mean_old + (1.0 - beta_first) * clipped
    new_var = beta_second * var_old + (1.0 - beta_second) * clipped * clipped
    mean_hat = new_mean / (1.0 - beta_first**STEP)
    var_hat = new_var / (1.0 - beta_second**STEP)
    updated = weights - learn_rate * (mean_hat / (jnp.sqrt(var_hat) + adam_eps) + decay * weights)
    return (clipped, new_var, updated)


def approx_inverse(tokens_low, scale):
    factor = dot("td,te->de", tokens_low, tokens_low) * scale
    order = factor.shape[0]
    top = jnp.max(jnp.sum(jnp.abs(factor), -1)) + 1e-06
    eye = jnp.eye(order, dtype=f32)
    shifted = factor / top + damping * eye
    start = 2.0 / kappa * eye - shifted / (kappa * kappa)
    start_low = start.astype(bf16)
    product = dot("ij,jk->ik", shifted.astype(bf16), start_low).astype(bf16)
    return 2.0 * start - dot("ij,jk->ik", product, start_low)


def series():
    alpha = 2.0 / kappa - damping / (kappa * kappa)
    beta = 1.0 / (kappa * kappa)
    return (
        2.0 * alpha - damping * alpha * alpha,
        -2.0 * beta - alpha * alpha + 2.0 * alpha * beta * damping,
        2.0 * alpha * beta - damping * beta * beta,
        -beta * beta,
    )


def sum_half(partial, core_bit):
    rows = partial.shape[0]
    halves = partial.reshape(2, rows // 2, partial.shape[1])
    keep = lax.dynamic_index_in_dim(halves, core_bit, 0, False)
    send = lax.dynamic_index_in_dim(halves, 1 - core_bit, 0, False)
    keep = keep + xor_permute(send, "blk", 1)
    return keep + xor_permute(keep, "blk", 2)


def join_half(half, core_bit):
    other = xor_permute(half, "blk", 1)
    both = by_order(core_bit, half, other, 0)
    return both.reshape((2 * half.shape[0],) + half.shape[1:])


def split_dots(left_low, right):
    high = right.astype(bf16)
    rest = (right - high.astype(f32)).astype(bf16)
    return jnp.dot(left_low, high, preferred_element_type=f32) + jnp.dot(
        left_low, rest, preferred_element_type=f32
    )


def body(
    token_ids,
    lengths,
    embedding,
    emb_mean,
    emb_var,
    positions,
    pos_mean,
    pos_var,
    gains_biases,
    gains_mean,
    gains_var,
    w_attn,
    attn_mean,
    attn_var,
    w_fc,
    fc_mean,
    fc_var,
    w_proj,
    proj_mean,
    proj_var,
):
    row_len = token_ids.shape[1]
    piece_rows = embedding.shape[0]
    dp_size = lax.axis_size("dp")
    blk_size = lax.axis_size("blk")
    dp_index = lax.axis_index("dp")
    blk_index = lax.axis_index("blk")
    core_bit = blk_index % 2
    chip_bit = blk_index // 2
    tokens = float(row_len * dp_size)
    sub_len = row_len // blk_size
    half_len = row_len // 2
    total_rows = row_len * dp_size
    ff_part = FF // blk_size
    head_cols = D // blk_size
    col_part = D // dp_size
    wide_part = FF // dp_size

    packed = spread(jnp.concatenate([token_ids[0], lengths[0]]), "dp")
    every_ids = packed[:, :row_len]
    every_lengths = packed[:, row_len:]
    every_local, every_counted, _ = jax.vmap(lambda row: doc_layout(row, row_len))(every_lengths)
    total_count = jnp.sum(every_counted.astype(f32))
    _, _, attn_mask = doc_layout(lengths[0], row_len)
    every_targets = jnp.concatenate([every_ids[:, 1:], jnp.zeros((dp_size, 1), jnp.int32)], 1)
    row_base = (dp_index * blk_size + blk_index) * piece_rows
    vocab_slots = row_base + jnp.arange(piece_rows, dtype=jnp.int32)
    table_low = embedding.astype(bf16)

    attn_low = w_attn[0].astype(bf16)
    qkv_all = lax.all_gather(attn_low[:, :3], "dp", axis=0)
    out_all = lax.all_gather(attn_low[:, 3], "dp", axis=0)
    fc_all = lax.all_gather(w_fc[0].astype(bf16), "dp", axis=0)
    proj_all = lax.all_gather(w_proj[0].astype(bf16), "dp", axis=0)
    span = dp_size // blk_size

    def turn(value):
        grouped = value.reshape((blk_size, span) + value.shape[1:])
        return lax.all_to_all(grouped, "blk", split_axis=0, concat_axis=0)

    qkv_turn = turn(qkv_all)
    w_qkv = jnp.transpose(qkv_turn, (0, 2, 3, 1, 4)).reshape(D, 3, head_cols)
    fc_turn = turn(fc_all)
    w_up = jnp.transpose(fc_turn, (0, 2, 1, 3)).reshape(D, ff_part)
    w_out = jnp.transpose(out_all, (1, 0, 2)).reshape(head_cols, D)
    w_down = jnp.transpose(proj_all, (1, 0, 2)).reshape(ff_part, D)

    def sub_of(index):
        return (index % 2) * (blk_size // 2) + index // 2

    id_subs = every_ids.reshape(dp_size, blk_size, sub_len)

    def picked(step):
        ids = lax.dynamic_index_in_dim(id_subs, sub_of(blk_index ^ step), 1, False).reshape(-1)
        hit = (ids[:, None] == vocab_slots[None, :]).astype(bf16)
        return jnp.dot(hit, table_low, preferred_element_type=f32).astype(bf16)

    far = jnp.stack([picked(1), picked(3)])
    near = jnp.stack([picked(0), picked(2)])
    near = near + xor_permute(far, "blk", 1)
    embedded_sub = near[0] + xor_permute(near[1], "blk", 2)
    embedded_sub = lax.all_to_all(
        embedded_sub.reshape(dp_size, sub_len, D), "dp", split_axis=0, concat_axis=0
    )
    embedded_sub = jnp.sum(embedded_sub.astype(f32), 0).astype(bf16)
    embedded = by_order(chip_bit, embedded_sub, xor_permute(embedded_sub, "blk", 2), 0)
    embedded = embedded.reshape(half_len, D).astype(f32)
    my_local, my_counted, _ = doc_layout(lengths[0], row_len)
    half_start = core_bit * half_len
    local_half = lax.dynamic_slice_in_dim(my_local, half_start, half_len, 0)
    pos_hit = (local_half[:, None] == jnp.arange(row_len, dtype=jnp.int32)[None, :]).astype(f32)
    stream = embedded + jnp.dot(pos_hit, positions, precision=HIGHEST)

    gain_one, shift_one, bias_q, bias_v, bias_o, gain_two, shift_two = (
        gains_biases[k] for k in range(7)
    )
    ff_rows = FF // D
    bias_fc = gains_biases[7 : 7 + ff_rows].reshape(FF)
    bias_proj = gains_biases[7 + ff_rows]
    gain_fin = gains_biases[8 + ff_rows]
    shift_fin = gains_biases[9 + ff_rows]

    def cut(vector, width):
        return lax.dynamic_slice_in_dim(vector, blk_index * width, width, 0)

    normed = join_half(layer_norm(stream, gain_one, shift_one).astype(bf16), core_bit)
    bias_q_cut, bias_v_cut = cut(bias_q, head_cols), cut(bias_v, head_cols)
    qkv_bias = jnp.stack([bias_q_cut, jnp.zeros_like(bias_q_cut), bias_v_cut])
    qkv_low = (dot("sd,dke->ske", normed, w_qkv) + qkv_bias).astype(bf16)
    heads_here = head_cols // HDIM
    split = qkv_low.reshape(row_len, 3, heads_here, HDIM)
    score_scale = 1.0 / math.sqrt(HDIM)
    scores = dot("shd,thd->hst", split[:, 0], split[:, 1]) * score_scale
    probs = jax.nn.softmax(jnp.where(attn_mask[None], scores, -1e30), axis=-1)
    probs_low = probs.astype(bf16)
    mixed = dot("hst,thd->shd", probs_low, split[:, 2]).astype(bf16).reshape(row_len, head_cols)
    middle = stream + sum_half(jnp.dot(mixed, w_out, preferred_element_type=f32), core_bit) + bias_o

    normed_two_half = layer_norm(middle, gain_two, shift_two).astype(bf16)
    normed_two = join_half(normed_two_half, core_bit)
    hidden = jnp.dot(normed_two, w_up, preferred_element_type=f32) + cut(bias_fc, ff_part)
    active = jax.nn.gelu(hidden, approximate=True).astype(bf16)
    stream_out = (
        middle
        + sum_half(jnp.dot(active, w_down, preferred_element_type=f32), core_bit)
        + bias_proj
    )
    final_half = layer_norm(stream_out, gain_fin, shift_fin).astype(bf16)

    final_here = spread(final_half, "dp")
    final_pair = by_order(core_bit, final_here, xor_permute(final_here, "blk", 1), 1)
    final_all = final_pair.reshape(total_rows, D)
    logits = dot("sd,vd->sv", final_all, table_low)
    target_hit = every_targets.reshape(-1)[:, None] == vocab_slots[None, :]
    top_here = jnp.max(logits, 1)
    sum_here = jnp.sum(jnp.exp(logits - top_here[:, None]), 1)
    hit_here = jnp.sum(jnp.where(target_hit, logits, 0.0), 1)
    stats = spread(jnp.stack([top_here, sum_here, hit_here]), ("dp", "blk"))
    top_all = jnp.max(stats[:, 0], 0)
    sum_all = jnp.sum(stats[:, 1] * jnp.exp(stats[:, 0] - top_all[None]), 0)
    target_logit = jnp.sum(stats[:, 2], 0)
    log_total = top_all + jnp.log(sum_all)
    flat_counted = every_counted.reshape(-1)
    loss_sum = jnp.sum(
        jnp.where(
            flat_counted, log_total - target_logit + zloss_weight * log_total * log_total, 0.0
        )
    )
    row_weight = jnp.where(flat_counted, 1.0, 0.0) / total_count
    glog = (
        row_weight[:, None]
        * (
            (1.0 + 2.0 * zloss_weight * log_total)[:, None] * jnp.exp(logits - log_total[:, None])
            - target_hit.astype(f32)
        )
    ).astype(bf16)
    head_part = jnp.dot(glog, table_low, preferred_element_type=f32)
    head_part = head_part.reshape(dp_size, 2, half_len, D)
    head_keep = lax.dynamic_index_in_dim(head_part, core_bit, 1, False)
    head_send = lax.dynamic_index_in_dim(head_part, 1 - core_bit, 1, False)
    head_keep = head_keep + xor_permute(head_send, "blk", 1)
    head_keep = head_keep.reshape(dp_size, 2, sub_len, D)
    head_send = lax.dynamic_index_in_dim(head_keep, 1 - chip_bit, 1, False).astype(bf16)
    head_keep = lax.dynamic_index_in_dim(head_keep, chip_bit, 1, False)
    head_keep = head_keep + xor_permute(head_send, "blk", 2).astype(f32)
    head_rows = lax.all_to_all(head_keep.astype(bf16), "dp", split_axis=0, concat_axis=0)
    head_sub = jnp.sum(head_rows.astype(f32), 0)
    grad_final = by_order(chip_bit, head_sub, xor_permute(head_sub, "blk", 2), 0)
    grad_final = grad_final.reshape(half_len, D)
    table_grad = dot("sv,sd->vd", glog, final_all)

    grad_out, d_gain_fin, d_shift_fin = norm_back(stream_out, gain_fin, grad_final)
    grad_proj_half = grad_out.astype(bf16)
    grad_proj = join_half(grad_proj_half, core_bit)
    grad_active = dot("sd,fd->sf", grad_proj, w_down)
    _, gelu_pull = jax.vjp(lambda value: jax.nn.gelu(value, approximate=True), hidden)
    grad_fc = gelu_pull(grad_active)[0].astype(bf16)
    back_two = sum_half(dot("sf,df->sd", grad_fc, w_up), core_bit)
    back_middle, d_gain_two, d_shift_two = norm_back(middle, gain_two, back_two)
    grad_middle = grad_out + back_middle
    grad_attn_half = grad_middle.astype(bf16)
    grad_attn = join_half(grad_attn_half, core_bit)
    grad_mixed = (
        dot("se,de->sd", grad_attn, w_out).astype(bf16).reshape(row_len, heads_here, HDIM)
    )
    grad_value = dot("hst,shd->thd", probs_low, grad_mixed)
    grad_probs = dot("shd,thd->hst", grad_mixed, split[:, 2])
    grad_scores = (
        probs * (grad_probs - jnp.sum(grad_probs * probs, -1, keepdims=True))
    ).astype(bf16)
    grad_query = dot("hst,thd->shd", grad_scores, split[:, 1]) * score_scale
    grad_key = dot("hst,shd->thd", grad_scores, split[:, 0]) * score_scale
    grad_qkv = (
        jnp.stack([grad_query, grad_key, grad_value], 1)
        .reshape(row_len, 3, head_cols)
        .astype(bf16)
    )
    back_one = sum_half(dot("ske,dke->sd", grad_qkv, w_qkv), core_bit)
    back_stream, d_gain_one, d_shift_one = norm_back(stream, gain_one, back_one)
    grad_stream = grad_middle + back_stream
    grad_embed_half = grad_stream.astype(bf16)

    pair_blocks = jnp.stack([grad_qkv[:, 0], grad_qkv[:, 1], grad_qkv[:, 2], mixed], 0)
    pair_got = lax.all_to_all(pair_blocks, "blk", split_axis=0, concat_axis=0)
    pair_got = jnp.transpose(pair_got, (1, 0, 2)).reshape(row_len, D)
    last = blk_index == blk_size - 1
    in_side = lax.all_gather(jnp.where(last, pair_got, normed), "dp", axis=0).reshape(-1, D)
    out_side = lax.all_gather(jnp.where(last, grad_attn, pair_got), "dp", axis=0).reshape(-1, D)

    def wide_half(value):
        halves = value.reshape(2, half_len, ff_part)
        keep = lax.dynamic_index_in_dim(halves, core_bit, 0, False)
        send = lax.dynamic_index_in_dim(halves, 1 - core_bit, 0, False)
        pair = by_order(core_bit, keep, xor_permute(send, "blk", 1), 1)
        pair = pair.reshape(half_len, 2 * ff_part)
        both = by_order(chip_bit, pair, xor_permute(pair, "blk", 2), 1)
        return both.reshape(half_len, FF)

    wide_rows = jnp.where(chip_bit == 0, wide_half(active), wide_half(grad_fc))
    slim_rows = jnp.where(chip_bit == 0, grad_proj_half, normed_two_half)
    wide_mine = lax.all_gather(wide_rows, "dp", axis=0).reshape(-1, FF)
    slim_mine = lax.all_gather(slim_rows, "dp", axis=0).reshape(-1, D)
    wide_pair = jnp.concatenate([wide_mine, xor_permute(wide_mine, "blk", 1)], 0)
    slim_pair = jnp.concatenate([slim_mine, xor_permute(slim_mine, "blk", 1)], 0)

    out_scale = total_count * total_count / tokens
    in_scale = 1.0 / tokens

    inv_in = approx_inverse(in_side, in_scale)
    inv_out = approx_inverse(out_side, out_scale)
    col_start = dp_index * col_part
    right = lax.dynamic_slice_in_dim(inv_out, col_start, col_part, 1)
    turned = split_dots(out_side, right)
    grad_cols = jnp.dot(
        in_side.T.astype(f32), turned, precision=HIGHEST
    )
    pre_small = jnp.dot(inv_in, grad_cols, precision=HIGHEST)

    wide_scale = jnp.where(chip_bit == 0, in_scale, out_scale)
    slim_scale = jnp.where(chip_bit == 0, out_scale, in_scale)
    inv_slim = approx_inverse(slim_pair, slim_scale)
    gram = dot("tf,sf->ts", wide_pair, wide_pair)
    trace = jnp.sum(jnp.square(wide_pair.astype(f32)))
    gram_low = (gram * (1.0 / jnp.maximum(trace, 1e-30))).astype(bf16)
    part_rows = 256
    part_first = (dp_index * 2 + core_bit) % (FF // part_rows) * part_rows
    if 2 * dp_size * part_rows < FF:
        part_rows = FF // (2 * dp_size)
        part_first = (dp_index * 2 + core_bit) * part_rows
    wide_part_cols = lax.dynamic_slice_in_dim(wide_pair, part_first, part_rows, 1)
    row_sums = jnp.sum(jnp.abs(dot("ti,tj->ij", wide_part_cols, wide_pair)), 1)
    top_part = jnp.max(row_sums) * wide_scale
    tops = spread(jnp.full((8, 128), top_part, f32), ("dp", "blk"))[:, 0, 0]
    tops = jnp.max(tops.reshape(dp_size, 2, 2), (0, 2))
    wide_top = jnp.where(chip_bit == 0, tops[0], tops[1]) + 1e-06
    slim_cols = col_part // 2
    wide_cols = wide_part // 2
    slim_right = lax.dynamic_slice_in_dim(
        inv_slim, dp_index * col_part + core_bit * slim_cols, slim_cols, 1
    )
    start_slim = split_dots(slim_pair, slim_right)
    start_slim = jnp.pad(start_slim, ((0, 0), (0, wide_cols - slim_cols)))
    start_wide = lax.dynamic_slice_in_dim(
        wide_pair, dp_index * wide_part + core_bit * wide_cols, wide_cols, 1
    ).astype(f32)
    power = jnp.where(chip_bit == 0, start_slim, start_wide)
    ratio = trace * wide_scale / wide_top
    coef = series()
    total = coef[0] * power
    factor = 1.0
    for step in range(1, 4):
        power = jnp.dot(gram_low, power.astype(bf16), preferred_element_type=f32)
        factor = factor * ratio
        total = total + (coef[step] * factor) * power
    total_slim = total[:, :slim_cols]
    pre_down = jnp.dot(wide_pair.T.astype(f32), total_slim, precision=HIGHEST)
    pre_up = jnp.dot(
        inv_slim,
        jnp.dot(slim_pair.T.astype(f32), total, precision=HIGHEST),
        precision=HIGHEST,
    )
    pre_wide = jnp.where(
        chip_bit == 0,
        pre_down.reshape(blk_size, ff_part * slim_cols),
        pre_up.reshape(blk_size, head_cols * wide_cols),
    )
    squares = jnp.sum(pre_small * pre_small) + jnp.sum(pre_wide * pre_wide)
    sent = jnp.concatenate([pre_small.reshape(blk_size, head_cols * col_part), pre_wide], 1)
    got = lax.all_to_all(sent, "blk", split_axis=0, concat_axis=0)
    small_count = head_cols * col_part
    pre_attn = jnp.transpose(
        got[:, :small_count].reshape(blk_size, head_cols, col_part), (1, 0, 2)
    )[None]
    got_wide = got[:, small_count:]
    pre_proj = jnp.concatenate(
        [got_wide[k].reshape(ff_part, slim_cols) for k in range(2)], 1
    )[None]
    pre_fc = jnp.concatenate(
        [got_wide[k].reshape(head_cols, wide_cols) for k in range(2, 4)], 1
    )[None]

    embed_here = spread(grad_embed_half, "dp")
    embed_pair = by_order(core_bit, embed_here, xor_permute(embed_here, "blk", 1), 1)
    grad_embed = embed_pair.reshape(total_rows, D)
    id_hit = (vocab_slots[:, None] == every_ids.reshape(-1)[None, :]).astype(bf16)
    table_grad = table_grad + jnp.dot(id_hit, grad_embed, preferred_element_type=f32)
    pos_all = (
        jnp.arange(row_len, dtype=jnp.int32)[:, None] == every_local.reshape(-1)[None, :]
    ).astype(bf16)
    grad_pos = jnp.dot(pos_all, grad_embed, preferred_element_type=f32)

    lead = (chip_bit == 0).astype(f32)
    token_rows = lead * jnp.stack(
        [
            d_gain_one,
            d_shift_one,
            jnp.sum(grad_attn_half.astype(f32), 0),
            d_gain_two,
            d_shift_two,
            jnp.sum(grad_proj_half.astype(f32), 0),
            d_gain_fin,
            d_shift_fin,
        ]
    )

    def place(vector, width):
        return lax.dynamic_update_slice_in_dim(
            jnp.zeros((vector.shape[0] * blk_size,), f32), vector, blk_index * width, 0
        )

    qkv_sums = jnp.sum(grad_qkv.astype(f32), 0)
    small_part = jnp.concatenate(
        [
            token_rows[:2],
            place(qkv_sums[0], head_cols)[None],
            place(qkv_sums[2], head_cols)[None],
            token_rows[2:5],
            place(jnp.sum(grad_fc.astype(f32), 0), ff_part).reshape(ff_rows, D),
            token_rows[5:],
        ],
        0,
    )
    small_part = small_part + xor_permute(small_part, "blk", 1)
    small_part = small_part + xor_permute(small_part, "blk", 2)
    grad_small = jnp.sum(spread(small_part, "dp"), 0)

    squares = squares + jnp.sum(table_grad * table_grad)
    every_squares = spread(jnp.full((8, 128), squares, f32), ("dp", "blk"))[:, 0, 0]
    all_squares = (
        jnp.sum(every_squares) + jnp.sum(grad_small * grad_small) + jnp.sum(grad_pos * grad_pos)
    )
    grad_norm = jnp.sqrt(all_squares)
    clip_factor = clip_level / jnp.maximum(grad_norm, clip_level)
    emb_out = adam_update(embedding, emb_mean, emb_var, table_grad, clip_factor, weight_decay)
    pos_out = adam_update(positions, pos_mean, pos_var, grad_pos, clip_factor, weight_decay)
    gains_out = adam_update(gains_biases, gains_mean, gains_var, grad_small, clip_factor, 0.0)
    attn_out = adam_update(w_attn, attn_mean, attn_var, pre_attn, clip_factor, weight_decay)
    fc_out = adam_update(w_fc, fc_mean, fc_var, pre_fc, clip_factor, weight_decay)
    proj_out = adam_update(w_proj, proj_mean, proj_var, pre_proj, clip_factor, weight_decay)
    return (
        (loss_sum, total_count, grad_norm)
        + emb_out
        + pos_out
        + gains_out
        + attn_out
        + fc_out
        + proj_out
    )


def solution(mesh):
    token = P("dp", None)
    table = P(("dp", "blk"), None)
    attn = P(None, "blk", None, "dp")
    flat = P(None, "blk", "dp")
    return jax.shard_map(
        body,
        mesh=mesh,
        in_specs=(token,) * 2
        + (table,) * 3
        + (P(),) * 6
        + (attn,) * 3
        + (flat,) * 6,
        out_specs=(P(),) * 3 + (table,) * 3 + (P(),) * 6 + (attn,) * 3 + (flat,) * 6,
        check_vma=False,
    )
```

time: 3070 us -> 663 us (0.22)
  waiting for transfers between devices: 1720 us -> 153 us
  blocking collectives: 851 us -> 132 us
  matrix products: 226 us -> 118 us
  other arithmetic: 158 us -> 64.3 us
  starting transfers between devices: 2.29 us -> 93.3 us
    psum x4 -> x0, waiting for transfers between devices: 955 us -> none  [the longest x1 921 us: body(): lax.psum((jnp.stack([item[0] for item in col_list]), jnp.stack([item[1] f...]
    unnamed x1 -> x0, blocking collectives: 742 us -> none
    all_gather x9 -> x5, waiting for transfers between devices: 763 us -> 39.4 us  [the longest x1 26.4 us: body(): lax.all_gather(jnp.where(last, pair_got, normed), 'dp', axis=0)]
    dot_general x34 -> x42, matrix products: 223 us -> 117 us  [the longest x19 60 us: dot(): return jnp.einsum(spec, left, right, preferred_element_type=f32)]
    psum x2 -> x0, blocking collectives: 72.9 us -> none  [the longest x1 44.1 us: body(): lax.psum(local_squares, ('dp', 'blk')) + jnp.sum(grad_small * grad_small)]
    all_gather x4 -> x3, blocking collectives: 29.9 us -> 98.5 us  [the longest x1 44.9 us: body(): slim_mine = lax.all_gather(slim_rows, 'dp', axis=0).reshape(-1, D)]
    ppermute x0 -> x28, waiting for transfers between devices: none -> 61.2 us  [xor_permute(): return lax.ppermute(value, axis, [(k, k ^ bit) for k in range(size)])]
    all_to_all x0 -> x11, starting transfers between devices: none -> 52.7 us  [the longest x6 28.7 us: spread(): return lax.all_to_all(copies, axes, split_axis=0, concat_axis=0)]
  transfers between devices with their start and end apart: 14 -> 44, of which waited for: 11 -> 25; matrix products, arithmetic and copies ran while one was open for 30% -> 22% of each run, Pallas kernels for 0% -> 0%
where the time goes in v1:
time: 663 us; the launch traced here: 655 us
  waiting for transfers between devices  153 us (23%)
  blocking collectives  132 us (20%)
  matrix products  118 us (18%)
  starting transfers between devices  93.3 us (14%)
  local copies, waits for them, and re-layouts  66.2 us (10%)
  other arithmetic  64.3 us (10%)
  between operations  28 us (4%)
    ppermute x28, waiting for transfers between devices, xor_permute(): return lax.ppermute(value, axis, [(k, k ^ bit) for k in range(size)])  61.2 us
    dot_general x19, matrix products, dot(): return jnp.einsum(spec, left, right, preferred_element_type=f32)  60 us
    all_gather x1, blocking collectives, body(): slim_mine = lax.all_gather(slim_rows, 'dp', axis=0).reshape(-1, D)  44.9 us
    ppermute x28, starting transfers between devices, xor_permute(): return lax.ppermute(value, axis, [(k, k ^ bit) for k in range(size)])  40.2 us
    all_to_all x6, waiting for transfers between devices, spread(): return lax.all_to_all(copies, axes, split_axis=0, concat_axis=0)  30.7 us
    all_to_all x6, starting transfers between devices, spread(): return lax.all_to_all(copies, axes, split_axis=0, concat_axis=0)  28.7 us
    all_gather x1, blocking collectives, body(): qkv_all = lax.all_gather(attn_low[:, :3], 'dp', axis=0)  28.4 us
    all_gather x1, waiting for transfers between devices, body(): lax.all_gather(jnp.where(last, pair_got, normed), 'dp', axis=0)  26.4 us
  transfers between devices with their start and end apart: 44, of which 25 were waited for; matrix products, arithmetic and copies ran while one was open for 22% of the time, Pallas kernels for 0%

profile of v1, /device:TPU:1, one launch (start us, length us, event | category | flops | bytes accessed | tf_op | source)
XLA Modules:
  0.0 655.5 jit_solution(13732992103143832650)
XLA Ops:
  8.5 6.4 all-to-all-start
  30.7 28.4 %all-gather = bf16[1536,3,96]{2,0,1:T(8,128)(2,1)S(1)} all-gather(bf16[192,3,96]{2,0,1:T(8,128)(2,1)S(1)} %slice.181), channel_id=2, replica_groups=mesh['dp'=8,'blk'=4] {'dp'}, dimensions={0}, use_global_device_ids=true | all-gather | bytes 995328 | tf_op jit(solution)/shard_map/all_gather | solution.py:194
  59.9 3.5 all-to-all-start.1
  67.3 7.6 %all-to-all-done.1 = bf16[8,32,768]{2,1,0:T(8,128)(2,1)S(1)} async-done(((bf16[8,32,768]{2,1,0:T(8,128)(2,1)}), bf16[8,32,768]{2,1,0:T(8,128)(2,1)S(1)}, u32[]{:S(2)}, u32[]{:S(2)}) %all-to-all-start.1) | async-done | bytes 393248 | tf_op jit(solution)/shard_map/all_to_all | solution.py:225
  74.9 9.1 %all-to-all-start.2 = ((bf16[4,2,192,3,96]{2,4,1,3,0:T(8,128)(2,1)}), bf16[4,2,192,3,96]{2,4,1,3,0:T(8,128)(2,1)S(1)}, u32[]{:S(2)}, u32[]{:S(2)}) async-start(bf16[4,2,192,3,96]{2,4,1,3,0:T(8,128)(2,1)} %copy.309), calls=%async_computation.2 | async-start | bytes 2359296 | tf_op jit(solution)/shard_map/all_to_all | solution.py:202
  85.6 14.5 %collective-permute-done.2 = bf16[32,768]{1,0:T(8,128)(2,1)S(1)} collective-permute-done((bf16[32,768]{1,0:T(8,128)(2,1)S(1)}, bf16[32,768]{1,0:T(8,128)(2,1)S(1)}, u32[]{:S(2)}, u32[]{:S(2)}) %collective-permute-start.2) | collective-permute-done | bytes 49184 | tf_op jit(solution)/shard_map/ppermute | solution.py:35
  101.8 25.2 %all-gather.1 = bf16[1536,1,96]{2,0,1:T(8,128)(2,1)S(1)} all-gather(bf16[192,1,96]{2,0,1:T(8,128)(2,1)S(1)} %slice.185), channel_id=3, replica_groups=mesh['dp'=8,'blk'=4] {'dp'}, dimensions={0}, use_global_device_ids=true | all-gather | bytes 331776 | tf_op jit(solution)/shard_map/all_gather | solution.py:195
  134.6 6.2 collective-permute-start.4
  142.7 3.5 copy.315
  146.2 3.8 all-to-all-start.3
  155.0 10.0 %all-to-all-done.3 = bf16[4,2,192,384]{3,1,2,0:T(2,128)(2,1)S(1)} async-done(((bf16[4,2,192,384]{3,1,2,0:T(2,128)(2,1)}), bf16[4,2,192,384]{3,1,2,0:T(2,128)(2,1)S(1)}, u32[]{:S(2)}, u32[]{:S(2)}) %all-to-all-start.3) | async-done | bytes 1179680 | tf_op jit(solution)/shard_map/all_to_all | solution.py:202
  166.9 13.0 %all-gather.11.cloned.1.call-done = bf16[8,768,96]{1,2,0:T(8,128)(2,1)} async-done(((bf16[1,768,96]{1,2,0:T(8,128)(2,1)}), bf16[8,768,96]{1,2,0:T(8,128)(2,1)}) %all-gather.11.cloned.1.call-update) | async-done | bytes 1179664 | tf_op jit(solution)/shard_map/all_gather | solution.py:197
  186.0 4.9 collective-permute-done.8
  191.5 22.0 %all_to_all.76 = bf16[8,64,768]{2,1,0:T(8,128)(2,1)S(1)} all-to-all(bf16[8,64,768]{2,1,0:T(8,128)(2,1)S(1)} %broadcast_in_dim.68), channel_id=1, replica_groups=mesh['dp'=8,'blk'=4] {'dp'}, dimensions={0} | all-to-all | bytes 1572864 | tf_op jit(solution)/shard_map/all_to_all | solution.py:43
  226.2 4.5 all-to-all-start.5
  231.8 13.9 %all-to-all-done.5 = f32[32,3,1024]{2,1,0:T(4,128)} async-done(((f32[32,3,1024]{2,1,0:T(4,128)}), f32[32,3,1024]{2,1,0:T(4,128)}, u32[]{:S(2)}, u32[]{:S(2)}) %all-to-all-start.5) | async-done | bytes 393248 | tf_op jit(solution)/shard_map/all_to_all | solution.py:43
  249.1 8.0 %fusion.204 = f32[1024,768]{1,0:T(8,128)S(1)} fusion(bf16[1572,768]{1,0:T(8,128)(2,1)} %copy-done.11, f32[1024,1572]{0,1:T(8,128)} %copy-done.4, f32[1024]{0:T(1024)S(1)} %get-tuple-element.213, f32[1024]{0:T(1024)S(1)} %get-tuple-element.212, f32[1024]{0:T(1024)S(1)} %divide_bitcast_fusion, s32[1024]{0:T(1024)S(1)} %pad_bitcast_fusion, ...), kind=kOutput, calls=%fused_computation.391 | convolution fusion | flops 2483810304 | bytes 12021904 | tf_op jit(solution)/shard_map/dot_general | solution.py:300
  269.0 9.7 %collective-permute-done.11 = bf16[8,32,768]{2,1,0:T(8,128)(2,1)} collective-permute-done((bf16[8,32,768]{2,1,0:T(8,128)(2,1)}, bf16[8,32,768]{2,1,0:T(8,128)(2,1)}, u32[]{:S(2)}, u32[]{:S(2)}) %collective-permute-start.11) | collective-permute-done | bytes 393248 | tf_op jit(solution)/shard_map/ppermute | solution.py:35
  280.1 11.9 %all_to_all.77 = bf16[8,32,768]{2,1,0:T(8,128)(2,1)S(1)} all-to-all(bf16[8,32,768]{2,1,0:T(8,128)(2,1)S(1)} %fusion.98), channel_id=1, replica_groups=mesh['dp'=8,'blk'=4] {'dp'}, dimensions={0} | all-to-all | bytes 786432 | tf_op jit(solution)/shard_map/all_to_all | solution.py:309
  302.1 4.9 collective-permute-start.13
  316.2 5.2 collective-permute-done.15
  329.5 3.7 all-to-all-start.7
  333.5 4.1 all-to-all-done.7
  342.9 4.7 collective-permute-done.18
  347.6 4.2 collective-permute-done.20
  359.1 4.6 collective-permute-done.24
  365.0 3.5 all-to-all-start.9
  368.6 44.9 %all-gather.2 = bf16[512,768]{1,0:T(8,128)(2,1)S(1)} all-gather(bf16[64,768]{1,0:T(8,128)(2,1)S(1)} %copy-done.36), channel_id=4, replica_groups=mesh['dp'=8,'blk'=4] {'dp'}, dimensions={0}, use_global_device_ids=true | all-gather | bytes 884736 | tf_op jit(solution)/shard_map/all_gather | solution.py:365
  413.5 6.6 %collective-permute-start.22 = (bf16[512,768]{1,0:T(8,128)(2,1)S(1)}, bf16[512,768]{1,0:T(8,128)(2,1)}, u32[]{:S(2)}, u32[]{:S(2)}) collective-permute-start(bf16[512,768]{1,0:T(8,128)(2,1)S(1)} %all-gather.2), channel_id=1, source_target_pairs={{0,1},{1,0},{2,3},{3,2},{4,5},{5,4},{6,7},{7,6},{8,9},{9,8},{10,11... | collective-permute-start | bytes 2359304 | tf_op jit(solution)/shard_map/ppermute | solution.py:35
  429.5 3.7 all-to-all-start.11
  434.0 7.9 %multiply_subtract_fusion.1 = f32[768,768]{0,1:T(8,128)} fusion(f32[]{:T(128)S(6)} %add.541, f32[768,768]{0,1:T(8,128)} %get-tuple-element.279, f32[]{:T(128)S(6)} %select_n.393), kind=kOutput, calls=%fused_computation.34 | convolution fusion | flops 1832583168 | bytes 4718600 | tf_op jit(solution)/shard_map/ij,jk->ik/dot_general | solution.py:30
  444.9 10.9 %all-to-all-done.11 = f32[8,14,768]{2,1,0:T(8,128)S(1)} async-done(((f32[8,14,768]{2,1,0:T(8,128)}), f32[8,14,768]{2,1,0:T(8,128)S(1)}, u32[]{:S(2)}, u32[]{:S(2)}) %all-to-all-start.11) | async-done | bytes 344096 | tf_op jit(solution)/shard_map/all_to_all | solution.py:43
  461.3 6.9 %multiply_reduce_fusion.1 = (f32[]{:T(128)}, f32[1572,768]{1,0:T(8,128)}) fusion(f32[1572,768]{1,0:T(8,128)S(1)} %fusion.5, bf16[1024,768]{1,0:T(8,128)(2,1)S(1)} %bitcast.424, f32[1024,1572]{0,1:T(8,128)S(1)} %bitcast.404, f32[1024]{0:T(1024)S(1)} %copy-done.73, f32[1024]{0:T(1024)S(1)} %copy-done.93, f32[1024]{0:T(1024)S(1)} %copy-done.89, ...), kind=kOutput, calls=%fused_computation.19 | convolution fusion | flops 2487432192 | bytes 17692820 | tf_op jit(solution)/shard_map/sv,sd->vd/dot_general | solution.py:30
  476.4 3.7 fusion.94
  480.0 3.6 copy.334
  484.5 26.4 %all-gather.13.cloned.1.call-done = bf16[8,128,768]{2,1,0:T(8,128)(2,1)} async-done(((bf16[1,128,768]{2,1,0:T(8,128)(2,1)}), bf16[8,128,768]{2,1,0:T(8,128)(2,1)}) %all-gather.13.cloned.1.call-update) | async-done | bytes 1572880 | tf_op jit(solution)/shard_map/all_gather | solution.py:350
  510.9 4.8 abs_reduce_fusion.2
  523.5 6.9 %fusion.60 = f32[768,768]{0,1:T(8,128)} fusion(f32[768,768,1]{0,1,2:T(8,128)} %get-tuple-element.275, f32[]{:T(128)S(6)} %add.535), kind=kOutput, calls=%fused_computation.78 | convolution fusion | flops 1826684928 | bytes 4718596 | tf_op jit(solution)/shard_map/ij,jk->ik/dot_general | solution.py:30
  530.4 5.6 multiply_reduce_fusion.4
  539.9 5.2 multiply_reduce_fusion
  546.4 3.9 fusion.23
  552.2 4.6 all-to-all-start.8
  556.9 9.6 %multiply_convert_fusion = bf16[1024,1024]{1,0:T(8,128)(2,1)S(1)} fusion(f32[]{:T(128)S(6)} %div.263, bf16[512,3072]{0,1:T(8,128)(2,1)} %collective-permute-done.21, bf16[512,3072]{0,1:T(8,128)(2,1)S(1)} %copy.334), kind=kOutput, calls=%fused_computation.20 | convolution fusion | flops 6457131008 | bytes 8388612 | tf_op jit(solution)/shard_map/tf,sf->ts/dot_general | solution.py:30
  579.0 5.0 fusion.227
  591.7 8.9 %multiply_reduce_fusion.2 = (f32[]{:T(128)}, f32[3072,48]{0,1:T(8,128)}) fusion(f32[3072,48]{0,1:T(8,128)} %copy.336, pred[]{:T(512)S(6)} %eq.93, f32[1024,192]{0,1:T(8,128)} %copy-done.9, bf16[512,3072]{0,1:T(8,128)(2,1)} %collective-permute-done.21, bf16[512,3072]{0,1:T(8,128)(2,1)S(1)} %copy.334), kind=kOutput, calls=%fused_computation.126 | convolution fusion | flops 1824964608 | bytes 7667717 | tf_op jit(solution)/shard_map/dot_general | solution.py:419
  603.2 6.0 all-to-all-start.10
  617.4 4.0 all-to-all-start.12
  624.2 12.9 %multiply_subtract_fusion = (f32[1572,768]{1,0:T(8,128)}, f32[1572,768]{1,0:T(8,128)}, f32[1572,768]{1,0:T(8,128)}) fusion(f32[1572,768]{1,0:T(8,128)} %param.22, f32[1572,768]{1,0:T(8,128)} %param.23, f32[1572,768]{1,0:T(8,128)} %param.24, f32[1572,768]{1,0:T(8,128)} %get-tuple-element.283, f32[]{:T(128)S(6)} %div.266), kind=kLoop, calls=%fused_computation.18 | loop fusion | flops 19316736 | bytes 33804292 | tf_op jit(solution)/shard_map/sub | solution.py:93
  (512 shorter events, 194.6 us)
Async XLA Ops:
  8.5 11.8 %all-to-all-start = ((s32[8,1,144]{2,1,0:T(1,128)}), s32[8,1,144]{2,1,0:T(1,128)S(1)}, u32[]{:S(2)}, u32[]{:S(2)}) async-start(s32[8,1,144]{2,1,0:T(1,128)} %broadcast_in_dim.62), calls=%async_computation | async-start | bytes 16384 | tf_op jit(solution)/shard_map/all_to_all | solution.py:43
  14.9 127.9 %all-gather.9.cloned.1.call-start = ((), (), s32[]{:S(2)}) async-start(), calls=%async_computation.13 | async-start | bytes 1327104 | tf_op jit(solution)/shard_map/all_gather | solution.py:196
  23.1 4.2 collective-permute-start
  28.7 30.4 %collective-permute-start.1 = (bf16[256,768]{1,0:T(8,128)(2,1)S(1)}, bf16[256,768]{1,0:T(8,128)(2,1)S(1)}, u32[]{:S(2)}, u32[]{:S(2)}) collective-permute-start(bf16[256,768]{1,0:T(8,128)(2,1)S(1)} %slice_bitcast_fusion), channel_id=1, source_target_pairs={{0,2},{1,3},{2,0},{3,1},{4,6},{5,7},{6,4},{7,5},{8,10},{9,11},{10,... | collective-permute-start | bytes 1179656 | tf_op jit(solution)/shard_map/ppermute | solution.py:35
  59.9 15.1 %all-to-all-start.1 = ((bf16[8,32,768]{2,1,0:T(8,128)(2,1)}), bf16[8,32,768]{2,1,0:T(8,128)(2,1)S(1)}, u32[]{:S(2)}, u32[]{:S(2)}) async-start(bf16[8,32,768]{2,1,0:T(8,128)(2,1)} %bitcast.8), calls=%async_computation.1 | async-start | bytes 786432 | tf_op jit(solution)/shard_map/all_to_all | solution.py:225
  64.0 36.7 %copy-start.52 = (f32[768]{0:T(1024)}, f32[768]{0:T(1024)S(1)}, u32[]{:S(2)}) copy-start(f32[768]{0:T(1024)S(1)} %get-tuple-element.172) | copy-start | bytes 9220
  74.9 53.4 %all-to-all-start.2 = ((bf16[4,2,192,3,96]{2,4,1,3,0:T(8,128)(2,1)}), bf16[4,2,192,3,96]{2,4,1,3,0:T(8,128)(2,1)S(1)}, u32[]{:S(2)}, u32[]{:S(2)}) async-start(bf16[4,2,192,3,96]{2,4,1,3,0:T(8,128)(2,1)} %copy.309), calls=%async_computation.2 | async-start | bytes 2359296 | tf_op jit(solution)/shard_map/all_to_all | solution.py:202
  84.0 95.8 %all-gather.11.cloned.1.call-start = ((), (), s32[]{:S(2)}) async-start(), calls=%async_computation.14 | async-start | bytes 1327104 | tf_op jit(solution)/shard_map/all_gather | solution.py:197
  84.1 16.0 %collective-permute-start.2 = (bf16[32,768]{1,0:T(8,128)(2,1)S(1)}, bf16[32,768]{1,0:T(8,128)(2,1)S(1)}, u32[]{:S(2)}, u32[]{:S(2)}) collective-permute-start(bf16[32,768]{1,0:T(8,128)(2,1)S(1)} %reduce_sum.478), channel_id=1, source_target_pairs={{0,2},{1,3},{2,0},{3,1},{4,6},{5,7},{6,4},{7,5},{8,10},{9,11},{10,... | collective-permute-start | bytes 147464 | tf_op jit(solution)/shard_map/ppermute | solution.py:35
  100.9 29.6 %collective-permute-start.3 = (bf16[64,768]{1,0:T(8,128)(2,1)S(1)}, bf16[64,768]{1,0:T(8,128)(2,1)S(1)}, u32[]{:S(2)}, u32[]{:S(2)}) collective-permute-start(bf16[64,768]{1,0:T(8,128)(2,1)S(1)} %add_convert_fusion.4), channel_id=1, source_target_pairs={{0,1},{1,0},{2,3},{3,2},{4,5},{5,4},{6,7},{7,6},{8,9},{9,8},{10,11... | collective-permute-start | bytes 294920 | tf_op jit(solution)/shard_map/ppermute | solution.py:35
  134.6 7.9 %collective-permute-start.4 = (f32[64,768]{1,0:T(8,128)S(1)}, f32[64,768]{1,0:T(8,128)S(1)}, u32[]{:S(2)}, u32[]{:S(2)}) collective-permute-start(f32[64,768]{1,0:T(8,128)S(1)} %dynamic-slice_bitcast_fusion.4), channel_id=1, source_target_pairs={{0,1},{1,0},{2,3},{3,2},{4,5},{5,4},{6,7},{7,6},{8,9},{9,8},{10,11... | collective-permute-start | bytes 589832 | tf_op jit(solution)/shard_map/ppermute | solution.py:35
  142.6 7.5 %collective-permute-start.5 = (f32[64,768]{1,0:T(8,128)S(1)}, f32[64,768]{1,0:T(8,128)S(1)}, u32[]{:S(2)}, u32[]{:S(2)}) collective-permute-start(f32[64,768]{1,0:T(8,128)S(1)} %bitcast_add_fusion.6), channel_id=1, source_target_pairs={{0,2},{1,3},{2,0},{3,1},{4,6},{5,7},{6,4},{7,5},{8,10},{9,11},{10,... | collective-permute-start | bytes 589832 | tf_op jit(solution)/shard_map/ppermute | solution.py:35
  146.2 18.8 %all-to-all-start.3 = ((bf16[4,2,192,384]{3,1,2,0:T(2,128)(2,1)}), bf16[4,2,192,384]{3,1,2,0:T(2,128)(2,1)S(1)}, u32[]{:S(2)}, u32[]{:S(2)}) async-start(bf16[4,2,192,384]{3,1,2,0:T(2,128)(2,1)} %copy.315), calls=%async_computation.3 | async-start | bytes 2359296 | tf_op jit(solution)/shard_map/all_to_all | solution.py:202
  152.6 1.6 collective-permute-start.6
  181.7 3.1 collective-permute-start.7
  184.8 6.2 collective-permute-start.8
  213.5 3.9 collective-permute-start.9
  226.2 19.5 %all-to-all-start.5 = ((f32[32,3,1024]{2,1,0:T(4,128)}), f32[32,3,1024]{2,1,0:T(4,128)}, u32[]{:S(2)}, u32[]{:S(2)}) async-start(f32[32,3,1024]{2,1,0:T(4,128)} %broadcast_in_dim.70), calls=%async_computation.5 | async-start | bytes 1048576 | tf_op jit(solution)/shard_map/all_to_all | solution.py:43
  260.1 4.0 collective-permute-start.10
  268.1 10.6 %collective-permute-start.11 = (bf16[8,32,768]{2,1,0:T(8,128)(2,1)}, bf16[8,32,768]{2,1,0:T(8,128)(2,1)}, u32[]{:S(2)}, u32[]{:S(2)}) collective-permute-start(bf16[8,32,768]{2,1,0:T(8,128)(2,1)} %fusion.114), channel_id=1, source_target_pairs={{0,2},{1,3},{2,0},{3,1},{4,6},{5,7},{6,4},{7,5},{8,10},{9,11},{10,... | collective-permute-start | bytes 1179656 | tf_op jit(solution)/shard_map/ppermute | solution.py:35
  292.0 3.5 collective-permute-start.12
  302.1 6.5 collective-permute-start.13
  313.4 1.5 collective-permute-start.14
  315.0 6.4 collective-permute-start.15
  322.9 1.9 collective-permute-start.16
  329.5 8.2 %all-to-all-start.7 = ((bf16[4,128,192]{1,2,0:T(8,128)(2,1)}), bf16[4,128,192]{1,2,0:T(8,128)(2,1)S(1)}, u32[]{:S(2)}, u32[]{:S(2)}) async-start(bf16[4,128,192]{1,2,0:T(8,128)(2,1)} %pad_maximum_fusion.9), calls=%async_computation.7 | async-start | bytes 393216 | tf_op jit(solution)/shard_map/all_to_all | solution.py:347
  333.2 136.8 %all-gather.15.cloned.1.call-start = ((), (), s32[]{:S(2)}) async-start(), calls=%async_computation.16 | async-start | bytes 1769472 | tf_op jit(solution)/shard_map/all_gather | solution.py:351
  338.5 141.5 %all-gather.17.cloned.1.call-start = ((), (), s32[]{:S(2)}) async-start(), calls=%async_computation.17 | async-start | bytes 3538944 | tf_op jit(solution)/shard_map/all_gather | solution.py:364
  338.8 1.9 collective-permute-start.17
  340.7 1.4 collective-permute-start.19
  341.2 6.4 collective-permute-start.18
  342.2 9.7 %collective-permute-start.20 = (bf16[64,1536]{1,0:T(8,128)(2,1)S(1)}, bf16[64,1536]{1,0:T(8,128)(2,1)S(1)}, u32[]{:S(2)}, u32[]{:S(2)}) collective-permute-start(bf16[64,1536]{1,0:T(8,128)(2,1)S(1)} %bitcast.443), channel_id=1, source_target_pairs={{0,2},{1,3},{2,0},{3,1},{4,6},{5,7},{6,4},{7,5},{8,10},{9,11},{10,... | collective-permute-start | bytes 589832 | tf_op jit(solution)/shard_map/ppermute | solution.py:35
  355.4 2.1 collective-permute-start.23
  357.5 6.2 collective-permute-start.24
  359.1 61.1 %copy-start.90 = (f32[768]{0:T(1024)S(1)}, f32[768]{0:T(1024)}, u32[]{:S(2)}) copy-start(f32[768]{0:T(1024)} %get-tuple-element.200) | copy-start | bytes 9220
  364.1 56.3 %copy-start.67 = (f32[768]{0:T(1024)S(1)}, f32[768]{0:T(1024)}, u32[]{:S(2)}) copy-start(f32[768]{0:T(1024)} %get-tuple-element.207) | copy-start | bytes 9220
  364.1 56.4 %copy-start.65 = (f32[768]{0:T(1024)S(1)}, f32[768]{0:T(1024)}, u32[]{:S(2)}) copy-start(f32[768]{0:T(1024)} %get-tuple-element.157) | copy-start | bytes 9220
  365.0 63.6 %all-to-all-start.9 = ((bf16[8,64,768]{2,1,0:T(8,128)(2,1)}), bf16[8,64,768]{2,1,0:T(8,128)(2,1)S(1)}, u32[]{:S(2)}, u32[]{:S(2)}) async-start(bf16[8,64,768]{2,1,0:T(8,128)(2,1)} %broadcast_in_dim.75), calls=%async_computation.9 | async-start | bytes 1572864 | tf_op jit(solution)/shard_map/all_to_all | solution.py:43
  368.6 142.3 %all-gather.13.cloned.1.call-start = ((), (), s32[]{:S(2)}) async-start(), calls=%async_computation.15 | async-start | bytes 1769472 | tf_op jit(solution)/shard_map/all_gather | solution.py:350
  413.5 8.7 %collective-permute-start.22 = (bf16[512,768]{1,0:T(8,128)(2,1)S(1)}, bf16[512,768]{1,0:T(8,128)(2,1)}, u32[]{:S(2)}, u32[]{:S(2)}) collective-permute-start(bf16[512,768]{1,0:T(8,128)(2,1)S(1)} %all-gather.2), channel_id=1, source_target_pairs={{0,1},{1,0},{2,3},{3,2},{4,5},{5,4},{6,7},{7,6},{8,9},{9,8},{10,11... | collective-permute-start | bytes 2359304 | tf_op jit(solution)/shard_map/ppermute | solution.py:35
  422.2 1.3 collective-permute-start.26
  423.5 5.2 collective-permute-start.27
  429.5 26.3 %all-to-all-start.11 = ((f32[8,14,768]{2,1,0:T(8,128)}), f32[8,14,768]{2,1,0:T(8,128)S(1)}, u32[]{:S(2)}, u32[]{:S(2)}) async-start(f32[8,14,768]{2,1,0:T(8,128)} %broadcast_in_dim.80), calls=%async_computation.11 | async-start | bytes 786432 | tf_op jit(solution)/shard_map/all_to_all | solution.py:43
  433.1 23.2 %collective-permute-start.25 = (bf16[8,64,768]{2,1,0:T(8,128)(2,1)S(1)}, bf16[8,64,768]{2,1,0:T(8,128)(2,1)}, u32[]{:S(2)}, u32[]{:S(2)}) collective-permute-start(bf16[8,64,768]{2,1,0:T(8,128)(2,1)S(1)} %all-to-all-done.9), channel_id=1, source_target_pairs={{0,1},{1,0},{2,3},{3,2},{4,5},{5,4},{6,7},{7,6},{8,9},{9,8},{10,11... | collective-permute-start | bytes 2359304 | tf_op jit(solution)/shard_map/ppermute | solution.py:35
  483.6 56.3 %collective-permute-start.21 = (bf16[512,3072]{0,1:T(8,128)(2,1)S(1)}, bf16[512,3072]{0,1:T(8,128)(2,1)}, u32[]{:S(2)}, u32[]{:S(2)}) collective-permute-start(bf16[512,3072]{0,1:T(8,128)(2,1)S(1)} %copy.334), channel_id=1, source_target_pairs={{0,1},{1,0},{2,3},{3,2},{4,5},{5,4},{6,7},{7,6},{8,9},{9,8},{10,11... | collective-permute-start | bytes 9437192 | tf_op jit(solution)/shard_map/ppermute | solution.py:35
  552.2 19.0 %all-to-all-start.8 = ((f32[32,8,128]{2,1,0:T(8,128)}), f32[32,8,128]{2,1,0:T(8,128)S(1)}, u32[]{:S(2)}, u32[]{:S(2)}) async-start(f32[32,8,128]{2,1,0:T(8,128)} %broadcast_in_dim_broadcast_in_dim_broadcast_in_dim.6), calls=%async_computation.8 | async-start | bytes 262144 | tf_op jit(solution)/shard_map/all_to_all | solution.py:43
  603.2 14.2 %all-to-all-start.10 = ((f32[32,8,128]{2,1,0:T(8,128)}), f32[32,8,128]{2,1,0:T(8,128)S(1)}, u32[]{:S(2)}, u32[]{:S(2)}) async-start(f32[32,8,128]{2,1,0:T(8,128)} %broadcast_in_dim_broadcast_in_dim_broadcast_in_dim.7), calls=%async_computation.10 | async-start | bytes 262144 | tf_op jit(solution)/shard_map/all_to_all | solution.py:43
  617.4 21.5 %all-to-all-start.12 = ((f32[4,1,55296]{2,1,0:T(1,128)}), f32[4,1,55296]{2,1,0:T(1,128)S(1)}, u32[]{:S(2)}, u32[]{:S(2)}) async-start(f32[4,1,55296]{2,1,0:T(1,128)} %copy.346), calls=%async_computation.12 | async-start | bytes 1769472 | tf_op jit(solution)/shard_map/all_to_all | solution.py:432
  (94 other events, 810.8 us)
Sparse Core Ops, SparseCore 0:
  30.8 45.7 all-gather.8
  142.6 37.1 all-gather.10
  338.7 54.9 all-gather.14
  396.3 69.5 all-gather.16
  468.5 42.3 all-gather.12

commit v2 on v1

v2 whole, which is shorter than its diff:
```python
import functools
import math

import jax
import jax.numpy as jnp
from jax import lax
from jax.experimental import pallas as pl
from jax.experimental.pallas import tpu as pltpu
from jax.sharding import PartitionSpec as P

D = 768
HEADS = 12
HDIM = 64
FF = 3072
STEP = 10

HIGHEST = lax.Precision.HIGHEST
ln_eps = 1e-05
zloss_weight = 0.01
damping = 0.1
clip_level = 0.02
learn_rate = 0.1
beta_first = 0.9
beta_second = 0.95
adam_eps = 1e-08
weight_decay = 0.1
kappa = 1.0 + damping
bf16 = jnp.bfloat16
f32 = jnp.float32


def dot(spec, left, right):
    return jnp.einsum(spec, left, right, preferred_element_type=f32)


def xor_permute(value, axis, bit):
    size = lax.axis_size(axis)
    return lax.ppermute(value, axis, [(k, k ^ bit) for k in range(size)])


def spread(value, axes):
    count = 1
    for name in axes if isinstance(axes, tuple) else (axes,):
        count *= lax.axis_size(name)
    copies = jnp.broadcast_to(value[None], (count,) + value.shape)
    return lax.all_to_all(copies, axes, split_axis=0, concat_axis=0)


def spread_small(value, axis):
    size = lax.axis_size(axis)
    index = lax.axis_index(axis)
    found = jnp.stack([value] + [xor_permute(value, axis, k) for k in range(1, size)])
    bits = size.bit_length() - 1
    found = found.reshape((2,) * bits + value.shape)
    for place in range(bits):
        bit = index // 2 ** (bits - 1 - place) % 2
        found = jnp.where(bit == 0, found, jnp.flip(found, place))
    return found.reshape((size,) + value.shape)


def gather_half(value):
    mine = spread(value, "dp").reshape(-1, value.shape[-1])
    return mine, xor_permute(mine, "blk", 1)


def together(*values):
    return lax.optimization_barrier(values)


def by_order(bit, mine, other, axis):
    first = jnp.where(bit == 0, mine, other)
    second = jnp.where(bit == 0, other, mine)
    return jnp.stack([first, second], axis)


def layer_norm(values, gain_vec, shift_vec):
    centered = values - jnp.mean(values, -1, keepdims=True)
    spread_val = jnp.mean(centered * centered, -1, keepdims=True)
    return centered * lax.rsqrt(spread_val + ln_eps) * gain_vec + shift_vec


def norm_back(values, gain_vec, cotangent):
    centered = values - jnp.mean(values, -1, keepdims=True)
    rstd = lax.rsqrt(jnp.mean(centered * centered, -1, keepdims=True) + ln_eps)
    unit = centered * rstd
    scaled = cotangent * gain_vec
    result = rstd * (
        scaled
        - jnp.mean(scaled, -1, keepdims=True)
        - unit * jnp.mean(scaled * unit, -1, keepdims=True)
    )
    return (
        result,
        jnp.sum(cotangent * unit, 0, keepdims=True),
        jnp.sum(cotangent, 0, keepdims=True),
    )


def doc_layout(lengths_row, row_len):
    doc_ends = jnp.cumsum(lengths_row, dtype=jnp.int32)
    spot_index = jnp.arange(row_len, dtype=jnp.int32)
    after_end = doc_ends[None, :] <= spot_index[:, None]
    segment = jnp.sum(after_end.astype(jnp.int32), 1, dtype=jnp.int32)
    start_pos = jnp.sum(jnp.where(after_end, lengths_row[None, :], 0), 1, dtype=jnp.int32)
    local_pos = spot_index - start_pos
    live_len = doc_ends[-1]
    next_seg = jnp.concatenate([segment[1:], jnp.full((1,), -1, jnp.int32)])
    counted = (spot_index + 1 < live_len) & (next_seg == segment)
    attn_mask = (spot_index[None, :] <= spot_index[:, None]) & (
        segment[None, :] == segment[:, None]
    )
    return (local_pos, counted, attn_mask)


def adam_update(weights, mean_old, var_old, gradient, clip_factor, decay):
    clipped = clip_factor * gradient
    new_mean = beta_first * mean_old + (1.0 - beta_first) * clipped
    new_var = beta_second * var_old + (1.0 - beta_second) * clipped * clipped
    mean_hat = new_mean / (1.0 - beta_first**STEP)
    var_hat = new_var / (1.0 - beta_second**STEP)
    updated = weights - learn_rate * (mean_hat / (jnp.sqrt(var_hat) + adam_eps) + decay * weights)
    return (clipped, new_var, updated)


def whole():
    return pl.BlockSpec(memory_space=pltpu.VMEM)


def scalar():
    return pl.BlockSpec(memory_space=pltpu.SMEM)


SMALL = pl.CostEstimate(flops=2**20, bytes_accessed=2**16, transcendentals=0)


def params(mib):
    return pltpu.CompilerParams(vmem_limit_bytes=mib * 2**20)


def turn_dot(left, right):
    return lax.dot_general(left, right, (((0,), (0,)), ((), ())), preferred_element_type=f32)


def far_dot(left, right):
    return lax.dot_general(left, right, (((1,), (1,)), ((), ())), preferred_element_type=f32)


def gelu_value(value):
    root = math.sqrt(2.0 / math.pi)
    square = value * value
    curve = jnp.tanh(value * (root + (root * 0.044715) * square))
    return value * (0.5 + 0.5 * curve)


def gelu_slope(value):
    root = math.sqrt(2.0 / math.pi)
    square = value * value
    curve = jnp.tanh(value * (root + (root * 0.044715) * square))
    bent = value * (root + (3.0 * root * 0.044715) * square)
    return 0.5 + 0.5 * (curve + (1.0 - curve * curve) * bent)


def add_product(total_ref, piece, fresh):
    product = far_dot(piece, piece)

    @pl.when(fresh)
    def _():
        total_ref[...] = product

    @pl.when(jnp.logical_not(fresh))
    def _():
        total_ref[...] += product


def wide_sums(share, first, total_ref, wide_ref, gram_ref, top_ref):
    top = jnp.maximum(jnp.max(jnp.abs(total_ref[...])), 1e-30)
    gram_ref[...] = (total_ref[...] * (1.0 / top)).astype(bf16)
    rows = wide_ref[:, pl.ds(pl.multiple_of(first, 128), share)]

    def sums(index, carry):
        outer = pl.ds(pl.multiple_of(index * 768, 768), 768)
        return carry + jnp.sum(jnp.abs(turn_dot(rows, wide_ref[:, outer])), 1, keepdims=True)

    row_sums = lax.fori_loop(0, wide_ref.shape[1] // 768, sums, jnp.zeros((share, 1), f32))
    top_ref[0] = top
    top_ref[1] = jnp.max(row_sums)


def wide_start_kernel(parts, step, spot_ref, bias_ref, in_ref, *refs):
    up_refs = refs[:parts]
    wide_ref = refs[parts]
    half = in_ref.shape[0] // 2
    width = up_refs[0].shape[1]

    def fill(bend):
        for part in range(parts):

            def columns(index, carry, part=part):
                inner = pl.ds(pl.multiple_of(index * step, step), step)
                outer = pl.ds(pl.multiple_of(part * width + index * step, step), step)
                for base in (0, half):
                    hidden = (
                        jnp.dot(
                            in_ref[base : base + half, :],
                            up_refs[part][:, inner],
                            preferred_element_type=f32,
                        )
                        + bias_ref[pl.ds(part, 1), inner]
                    )
                    wide_ref[base : base + half, outer] = bend(hidden).astype(bf16)
                return carry

            lax.fori_loop(0, width // step, columns, 0)

    @pl.when(spot_ref[0] == 0)
    def _():
        fill(gelu_value)

    @pl.when(spot_ref[0] != 0)
    def _():
        fill(gelu_slope)


def fits(rows):
    return rows <= 1024


def plain_wide_start(spot, bias, slim_in, ups):
    pieces = []
    for part, up in enumerate(ups):
        hidden = jnp.dot(slim_in, up, preferred_element_type=f32) + bias[part]
        pieces.append(jnp.where(spot[0] == 0, gelu_value(hidden), gelu_slope(hidden)).astype(bf16))
    return jnp.concatenate(pieces, 1)


def plain_wide_back(spot, start, slim_out, downs, share):
    back = jnp.concatenate([far_dot(slim_out, down) for down in downs], 1)
    wide = jnp.where(spot[0] == 0, start, (start.astype(f32) * back).astype(bf16))
    gram = far_dot(wide, wide)
    top = jnp.maximum(jnp.max(jnp.abs(gram)), 1e-30)
    rows = lax.dynamic_slice_in_dim(wide, spot[1], share, 1)
    sums = jnp.max(jnp.sum(jnp.abs(turn_dot(rows, wide)), 1))
    return wide, (gram * (1.0 / top)).astype(bf16), jnp.stack([top, sums])


def plain_wide_finish(chip, coefs, gram, start, wide, slim_in, left, columns):
    power, total = start, coefs[0] * start
    for step in range(1, 4):
        power = jnp.dot(gram, power.astype(bf16), preferred_element_type=f32)
        total = total + coefs[step] * power
    model = slim_in.shape[1]
    high, rest = high_low(total)
    down = jnp.stack(
        [
            (turn_dot(high, piece) + turn_dot(rest, piece))[:columns]
            for piece in (wide[:, :model], wide[:, model : 2 * model])
        ]
    )
    turned = turn_dot(slim_in, high) + turn_dot(slim_in, rest)
    up = jnp.dot(left, turned, precision=HIGHEST)
    square = jnp.where(chip[0] == 0, jnp.sum(down * down), jnp.sum(up * up))
    return down, up, square.reshape(1)


def wide_start(spot, bias, slim_in, ups):
    parts = len(ups)
    rows, total = slim_in.shape[0], parts * ups[0].shape[1]
    if not fits(rows):
        return plain_wide_start(spot, bias, slim_in, ups)
    return pl.pallas_call(
        functools.partial(wide_start_kernel, parts, 256),
        out_shape=jax.ShapeDtypeStruct((rows, total), bf16),
        in_specs=[scalar()] + [whole()] * (2 + parts),
        out_specs=whole(),
        compiler_params=params(48),
        cost_estimate=SMALL,
    )(spot, bias, slim_in, *ups)


def wide_back_kernel(parts, step, share, spot_ref, start_ref, out_ref, *refs):
    down_refs = refs[:parts]
    wide_ref, gram_ref, top_ref, total_ref = refs[parts:]
    half = out_ref.shape[0] // 2
    width = down_refs[0].shape[0]

    @pl.when(spot_ref[0] == 0)
    def _():
        wide_ref[...] = start_ref[...]

        def columns(index, carry):
            outer = pl.ds(pl.multiple_of(index * width, width), width)
            add_product(total_ref, start_ref[:, outer], index == 0)
            return carry

        lax.fori_loop(0, parts, columns, 0)

    @pl.when(spot_ref[0] != 0)
    def _():
        for part in range(parts):

            def columns(index, carry, part=part):
                inner = pl.ds(pl.multiple_of(index * step, step), step)
                outer = pl.ds(pl.multiple_of(part * width + index * step, step), step)
                for base in (0, half):
                    back = far_dot(out_ref[base : base + half, :], down_refs[part][inner, :])
                    slope = start_ref[base : base + half, outer].astype(f32)
                    wide_ref[base : base + half, outer] = (slope * back).astype(bf16)
                fresh = jnp.logical_and(part == 0, index == 0)
                add_product(total_ref, wide_ref[:, outer], fresh)
                return carry

            lax.fori_loop(0, width // step, columns, 0)

    wide_sums(share, spot_ref[1], total_ref, wide_ref, gram_ref, top_ref)


def wide_back(spot, start, slim_out, downs, share):
    rows, total = start.shape
    parts = len(downs)
    if not fits(rows):
        return plain_wide_back(spot, start, slim_out, downs, share)
    return pl.pallas_call(
        functools.partial(wide_back_kernel, parts, 384, share),
        out_shape=(
            jax.ShapeDtypeStruct((rows, total), bf16),
            jax.ShapeDtypeStruct((rows, rows), bf16),
            jax.ShapeDtypeStruct((2,), f32),
        ),
        in_specs=[scalar()] + [whole()] * (2 + parts),
        out_specs=(whole(), whole(), scalar()),
        scratch_shapes=[pltpu.VMEM((rows, rows), f32)],
        compiler_params=params(56),
        cost_estimate=SMALL,
    )(spot, start, slim_out, *downs)


def lane_row(ref, first, count):
    return jnp.concatenate([ref[first + k : first + k + 1, :] for k in range(count)], 1)


def head_kernel(
    limit, step, base_ref, target_ref, counted_ref, table_ref, one, two, logit_ref, log_ref, hit_ref
):
    half = one.shape[0]
    blocks = half // 128
    starts = jnp.full((1, half), -1e30, f32)

    def places(index):
        return lax.broadcasted_iota(jnp.int32, (step, 1), 0) + index * step

    def fill(index, tops):
        rows = pl.ds(pl.multiple_of(index * step, 16), step)
        result = []
        for part, ref in enumerate((one, two)):
            value = far_dot(table_ref[rows, :], ref[...])
            value = jnp.where(places(index) < limit, value, -1e30)
            logit_ref[rows, part * half : (part + 1) * half] = value
            result.append(jnp.maximum(tops[part], jnp.max(value, 0, keepdims=True)))
        return tuple(result)

    count = table_ref.shape[0] // step
    tops = lax.fori_loop(0, count, fill, (starts, starts))
    base = base_ref[0]
    goals = [lane_row(target_ref, part * blocks, blocks) - base for part in range(2)]
    zeros = jnp.zeros((1, half), f32)

    def add_up(index, carry):
        rows = pl.ds(pl.multiple_of(index * step, 16), step)
        place = places(index)
        result = []
        for part in range(2):
            value = logit_ref[rows, part * half : (part + 1) * half]
            total, hits = carry[part]
            total += jnp.sum(jnp.exp(value - tops[part]), 0, keepdims=True)
            found = jnp.logical_and(place == goals[part], place < limit)
            hits += jnp.sum(jnp.where(found, value, 0.0), 0, keepdims=True)
            result.append((total, hits))
        return tuple(result)

    sums = lax.fori_loop(0, count, add_up, ((zeros, zeros), (zeros, zeros)))
    hit_sum = jnp.float32(0.0)
    for part in range(2):
        total, hits = sums[part]
        log_total = tops[part] + jnp.log(total)
        for k in range(blocks):
            row = part * blocks + k
            log_ref[row : row + 1, :] = log_total[:, k * 128 : (k + 1) * 128]
        hit_sum += jnp.sum(hits * lane_row(counted_ref, part * blocks, blocks))
    hit_ref[0] = hit_sum


def head_logits(base, targets, counted, table, one, two, limit):
    rows = table.shape[0]
    tokens = 2 * one.shape[0]
    return pl.pallas_call(
        functools.partial(head_kernel, limit, rows // 8),
        out_shape=(
            jax.ShapeDtypeStruct((rows, tokens), f32),
            jax.ShapeDtypeStruct((tokens // 128, 128), f32),
            jax.ShapeDtypeStruct((1,), f32),
        ),
        in_specs=[scalar()] + [whole()] * 5,
        out_specs=(whole(), whole(), scalar()),
        compiler_params=params(40),
        cost_estimate=SMALL,
    )(base, targets, counted, table, one, two)


def head_back_kernel(
    limit,
    step,
    base_ref,
    target_ref,
    weight_ref,
    log_ref,
    table_ref,
    logit_ref,
    own_ref,
    far_ref,
    glog_ref,
):
    half = own_ref.shape[0]
    blocks = half // 128
    base = base_ref[0]
    for part in range(2):
        goal = lane_row(target_ref, part * blocks, blocks) - base
        weight = lane_row(weight_ref, part * blocks, blocks)
        log_total = lane_row(log_ref, part * blocks, blocks)
        factor = weight * (1.0 + 2.0 * zloss_weight * log_total)

        def fill(index, carry, part=part, goal=goal, weight=weight, log_total=log_total, factor=factor):
            rows = pl.ds(pl.multiple_of(index * step, 16), step)
            place = lax.broadcasted_iota(jnp.int32, (step, 1), 0) + index * step
            value = logit_ref[rows, part * half : (part + 1) * half]
            found = jnp.logical_and(place == goal, place < limit)
            grad = factor * jnp.exp(value - log_total) - jnp.where(found, weight, 0.0)
            glog_ref[rows, part * half : (part + 1) * half] = grad.astype(bf16)
            return carry

        lax.fori_loop(0, table_ref.shape[0] // step, fill, 0)
    for part, ref in ((1, far_ref), (0, own_ref)):
        for k in range(half // 256):
            spot = k * 256
            value = turn_dot(
                glog_ref[:, part * half + spot : part * half + spot + 256], table_ref[...]
            )
            ref[spot : spot + 256, :] = value.astype(ref.dtype)


def head_back(base, targets, weights, logs, table, logits, limit):
    rows, tokens = logits.shape
    model = table.shape[1]
    return pl.pallas_call(
        functools.partial(head_back_kernel, limit, rows // 8),
        out_shape=(
            jax.ShapeDtypeStruct((tokens // 2, model), f32),
            jax.ShapeDtypeStruct((tokens // 2, model), bf16),
            jax.ShapeDtypeStruct((rows, tokens), bf16),
        ),
        in_specs=[scalar()] + [whole()] * 5,
        out_specs=(whole(), whole(), whole()),
        compiler_params=params(48),
        cost_estimate=SMALL,
    )(base, targets, weights, logs, table, logits)


def high_low(value):
    high = value.astype(bf16)
    return high, (value - high.astype(f32)).astype(bf16)


def inverse_parts(token_refs, scale, out_ref, start_ref, shifted_ref):
    order = out_ref.shape[0]
    step = 256

    def gram_rows(index, top):
        rows = pl.ds(pl.multiple_of(index * step, step), step)
        value = jnp.zeros((step, order), f32)
        for ref in token_refs:
            value += turn_dot(ref[:, rows], ref[...])
        value = value * scale
        out_ref[rows, :] = value
        return jnp.maximum(top, jnp.max(jnp.sum(jnp.abs(value), 1)))

    top = lax.fori_loop(0, order // step, gram_rows, jnp.float32(0.0)) + 1e-06

    def start_rows(index, carry):
        rows = pl.ds(pl.multiple_of(index * step, step), step)
        place = lax.broadcasted_iota(jnp.int32, (step, order), 0) + index * step
        eye = (place == lax.broadcasted_iota(jnp.int32, (step, order), 1)).astype(f32)
        shifted = out_ref[rows, :] / top + damping * eye
        start = 2.0 / kappa * eye - shifted * (1.0 / (kappa * kappa))
        shifted_ref[rows, :] = shifted.astype(bf16)
        start_ref[rows, :] = start.astype(bf16)
        out_ref[rows, :] = 2.0 * start
        return carry

    lax.fori_loop(0, order // step, start_rows, 0)

    def last_rows(index, carry):
        rows = pl.ds(pl.multiple_of(index * step, step), step)
        product = jnp.dot(shifted_ref[rows, :], start_ref[...], preferred_element_type=f32)
        out_ref[rows, :] = out_ref[rows, :] - jnp.dot(
            product.astype(bf16), start_ref[...], preferred_element_type=f32
        )
        return carry

    lax.fori_loop(0, order // step, last_rows, 0)


def pick_columns(inverse_ref, first, lanes):
    order = inverse_ref.shape[0]
    place = lax.broadcasted_iota(jnp.int32, (order, lanes), 0) - first
    chosen = (place == lax.broadcasted_iota(jnp.int32, (order, lanes), 1)).astype(bf16)
    high, rest = high_low(inverse_ref[...])
    return (
        jnp.dot(high, chosen, preferred_element_type=f32).astype(bf16),
        jnp.dot(rest, chosen, preferred_element_type=f32).astype(bf16),
    )


def inverse_kernel(count, scale_ref, *refs):
    out_ref, start_ref, shifted_ref = refs[count:]
    inverse_parts(refs[:count], scale_ref[0], out_ref, start_ref, shifted_ref)


def slim_kernel(count, scale_ref, first_ref, *refs):
    token_refs = refs[:count]
    out_ref, turned_ref, start_ref, shifted_ref = refs[count:]
    inverse_parts(token_refs, scale_ref[0], out_ref, start_ref, shifted_ref)
    high, rest = pick_columns(out_ref, first_ref[0], turned_ref.shape[1])
    base = 0
    for ref in token_refs:
        rows = ref.shape[0]
        turned_ref[base : base + rows, :] = jnp.dot(
            ref[...], high, preferred_element_type=f32
        ) + jnp.dot(ref[...], rest, preferred_element_type=f32)
        base += rows


def pair_kernel(count, scale_ref, first_ref, left_ref, *refs):
    in_refs = refs[:count]
    token_refs = refs[count : 2 * count]
    result_ref, square_ref, out_ref, start_ref, shifted_ref = refs[2 * count :]
    lanes = 128
    inverse_parts(token_refs, scale_ref[0], out_ref, start_ref, shifted_ref)
    high, rest = pick_columns(out_ref, first_ref[0], lanes)
    order = out_ref.shape[0]
    grad = jnp.zeros((lanes, order), f32)
    for in_ref, ref in zip(in_refs, token_refs):
        turned = jnp.dot(ref[...], high, preferred_element_type=f32) + jnp.dot(
            ref[...], rest, preferred_element_type=f32
        )
        turned_high, turned_rest = high_low(turned)
        grad += turn_dot(turned_high, in_ref[...]) + turn_dot(turned_rest, in_ref[...])
    grad_high, grad_rest = high_low(grad)
    left_high, left_rest = high_low(left_ref[...])
    result = (
        far_dot(left_high, grad_high) + far_dot(left_rest, grad_high) + far_dot(left_high, grad_rest)
    )
    result = result[:, : result_ref.shape[1]]
    result_ref[...] = result
    square_ref[0] = jnp.sum(result * result)


def approx_inverse(parts, scale):
    order = parts[0].shape[1]
    count = len(parts)
    rows = sum(part.shape[0] for part in parts)
    return pl.pallas_call(
        functools.partial(inverse_kernel, count),
        out_shape=jax.ShapeDtypeStruct((order, order), f32),
        in_specs=[scalar()] + [whole()] * count,
        out_specs=whole(),
        scratch_shapes=[pltpu.VMEM((order, order), bf16)] * 2,
        compiler_params=params(40),
        cost_estimate=SMALL,
    )(scale, *parts)


def slim_inverse(parts, scale, first):
    order = parts[0].shape[1]
    count = len(parts)
    rows = sum(part.shape[0] for part in parts)
    return pl.pallas_call(
        functools.partial(slim_kernel, count),
        out_shape=(
            jax.ShapeDtypeStruct((order, order), f32),
            jax.ShapeDtypeStruct((rows, 128), f32),
        ),
        in_specs=[scalar()] * 2 + [whole()] * count,
        out_specs=(whole(), whole()),
        scratch_shapes=[pltpu.VMEM((order, order), bf16)] * 2,
        compiler_params=params(40),
        cost_estimate=SMALL,
    )(scale, first, *parts)


def pair_factor(in_parts, out_parts, left, scale, first, columns):
    order = left.shape[0]
    count = len(in_parts)
    rows = sum(part.shape[0] for part in in_parts)
    return pl.pallas_call(
        functools.partial(pair_kernel, count),
        out_shape=(
            jax.ShapeDtypeStruct((order, columns), f32),
            jax.ShapeDtypeStruct((1,), f32),
        ),
        in_specs=[scalar()] * 2 + [whole()] * (1 + 2 * count),
        out_specs=(whole(), scalar()),
        scratch_shapes=[pltpu.VMEM((order, order), f32)] + [pltpu.VMEM((order, order), bf16)] * 2,
        compiler_params=params(48),
        cost_estimate=SMALL,
    )(scale, first, left, *in_parts, *out_parts)


def finish_kernel(
    columns,
    chip_ref,
    coef_ref,
    gram_ref,
    start_ref,
    wide_ref,
    in_ref,
    left_ref,
    down_ref,
    up_ref,
    square_ref,
    total_ref,
    power_ref,
):
    power_ref[...] = start_ref[...]
    total_ref[...] = coef_ref[0] * start_ref[...]
    for step in range(1, 4):
        power_ref[...] = jnp.dot(
            gram_ref[...], power_ref[...].astype(bf16), preferred_element_type=f32
        )
        total_ref[...] += coef_ref[step] * power_ref[...]
    model = in_ref.shape[1]

    @pl.when(chip_ref[0] == 0)
    def _():
        high, rest = high_low(total_ref[:, :128])
        square = jnp.float32(0.0)
        for part in range(2):
            piece = wide_ref[:, part * model : (part + 1) * model]
            result = (turn_dot(high, piece) + turn_dot(rest, piece))[:columns, :]
            down_ref[part] = result
            square += jnp.sum(result * result)
        up_ref[...] = jnp.zeros_like(up_ref)
        square_ref[0] = square

    @pl.when(chip_ref[0] != 0)
    def _():
        high, rest = high_low(total_ref[...])
        turned = turn_dot(in_ref[...], high) + turn_dot(in_ref[...], rest)
        turned_high, turned_rest = high_low(turned)
        left_high, left_rest = high_low(left_ref[...])
        result = (
            jnp.dot(left_high, turned_high, preferred_element_type=f32)
            + jnp.dot(left_rest, turned_high, preferred_element_type=f32)
            + jnp.dot(left_high, turned_rest, preferred_element_type=f32)
        )
        up_ref[...] = result
        down_ref[...] = jnp.zeros_like(down_ref)
        square_ref[0] = jnp.sum(result * result)


def wide_finish(chip, coefs, gram, start, wide, slim_in, left, columns):
    rows, width = start.shape
    model = slim_in.shape[1]
    if not fits(rows):
        return plain_wide_finish(chip, coefs, gram, start, wide, slim_in, left, columns)
    return pl.pallas_call(
        functools.partial(finish_kernel, columns),
        out_shape=(
            jax.ShapeDtypeStruct((2, columns, model), f32),
            jax.ShapeDtypeStruct((left.shape[0], width), f32),
            jax.ShapeDtypeStruct((1,), f32),
        ),
        in_specs=[scalar()] * 2 + [whole()] * 5,
        out_specs=(whole(), whole(), scalar()),
        scratch_shapes=[pltpu.VMEM((rows, width), f32)] * 2,
        compiler_params=params(48),
        cost_estimate=SMALL,
    )(chip, coefs, gram, start, wide, slim_in, left)


def series():
    alpha = 2.0 / kappa - damping / (kappa * kappa)
    beta = 1.0 / (kappa * kappa)
    return (
        2.0 * alpha - damping * alpha * alpha,
        -2.0 * beta - alpha * alpha + 2.0 * alpha * beta * damping,
        2.0 * alpha * beta - damping * beta * beta,
        -beta * beta,
    )


def sum_half(partial, core_bit):
    rows = partial.shape[0]
    halves = partial.reshape(2, rows // 2, partial.shape[1])
    keep = lax.dynamic_index_in_dim(halves, core_bit, 0, False)
    send = lax.dynamic_index_in_dim(halves, 1 - core_bit, 0, False)
    keep = keep + xor_permute(send, "blk", 1)
    return keep + xor_permute(keep, "blk", 2)


def join_half(half, core_bit):
    other = xor_permute(half, "blk", 1)
    both = by_order(core_bit, half, other, 0)
    return both.reshape((2 * half.shape[0],) + half.shape[1:])


def split_dots(left_low, right):
    high = right.astype(bf16)
    rest = (right - high.astype(f32)).astype(bf16)
    return jnp.dot(left_low, high, preferred_element_type=f32) + jnp.dot(
        left_low, rest, preferred_element_type=f32
    )


def body(
    token_ids,
    lengths,
    embedding,
    emb_mean,
    emb_var,
    positions,
    pos_mean,
    pos_var,
    gains_biases,
    gains_mean,
    gains_var,
    w_attn,
    attn_mean,
    attn_var,
    w_fc,
    fc_mean,
    fc_var,
    w_proj,
    proj_mean,
    proj_var,
):
    row_len = token_ids.shape[1]
    piece_rows = embedding.shape[0]
    dp_size = lax.axis_size("dp")
    blk_size = lax.axis_size("blk")
    dp_index = lax.axis_index("dp")
    blk_index = lax.axis_index("blk")
    core_bit = blk_index % 2
    chip_bit = blk_index // 2
    row_bit = dp_index % 2
    tokens = float(row_len * dp_size)
    sub_len = row_len // blk_size
    half_len = row_len // 2
    total_rows = row_len * dp_size
    ff_part = FF // blk_size
    head_cols = D // blk_size
    col_part = D // dp_size
    wide_part = FF // dp_size

    packed = spread_small(jnp.concatenate([token_ids[0], lengths[0]]), "dp")
    every_ids = packed[:, :row_len]
    every_lengths = packed[:, row_len:]
    every_local, every_counted, _ = jax.vmap(lambda row: doc_layout(row, row_len))(every_lengths)
    total_count = jnp.sum(every_counted.astype(f32))
    _, _, attn_mask = doc_layout(lengths[0], row_len)
    every_targets = jnp.concatenate([every_ids[:, 1:], jnp.zeros((dp_size, 1), jnp.int32)], 1)
    row_base = (dp_index * blk_size + blk_index) * piece_rows
    vocab_slots = row_base + jnp.arange(piece_rows, dtype=jnp.int32)
    table_low = embedding.astype(bf16)

    span = dp_size // blk_size
    attn_low = w_attn[0].astype(bf16)
    rows_here = attn_low.shape[0]
    qkv_all = spread(attn_low[:, :3].reshape(rows_here, 3 * col_part), "dp")
    up_low = w_fc[0].astype(bf16)
    down_low = w_proj[0].astype(bf16).reshape(rows_here, wide_part)
    out_low = attn_low[:, 3].reshape(rows_here // 4, wide_part)
    mid_all = lax.all_gather(jnp.concatenate([up_low, out_low], 0), "dp", axis=0)
    down_all = lax.all_gather(down_low, "dp", axis=0)

    def turn(value):
        grouped = value.reshape((blk_size, span) + value.shape[1:])

        def block(index):
            return lax.dynamic_index_in_dim(grouped, index, 0, False)

        found = [block(blk_index)] + [
            xor_permute(block(blk_index ^ k), "blk", k) for k in range(1, blk_size)
        ]
        return jnp.stack(
            [
                jnp.where(
                    chip_bit == 0,
                    jnp.where(core_bit == 0, found[k], found[k ^ 1]),
                    jnp.where(core_bit == 0, found[k ^ 2], found[k ^ 3]),
                )
                for k in range(blk_size)
            ]
        )

    def sub_of(index):
        return (index % 2) * (blk_size // 2) + index // 2

    id_subs = every_ids.reshape(dp_size, blk_size, sub_len)

    def picked(step):
        ids = lax.dynamic_index_in_dim(id_subs, sub_of(blk_index ^ step), 1, False).reshape(-1)
        hit = (ids[:, None] == vocab_slots[None, :]).astype(bf16)
        return jnp.dot(hit, table_low, preferred_element_type=f32).astype(bf16)

    far = jnp.stack([picked(1), picked(3)])
    near = jnp.stack([picked(0), picked(2)])
    near = near + xor_permute(far, "blk", 1)
    embedded_sub = near[0] + xor_permute(near[1], "blk", 2)
    embedded_sub, qkv_all = together(embedded_sub, qkv_all)
    qkv_turn = turn(qkv_all).reshape(blk_size, span, rows_here, 3, col_part)
    w_qkv = jnp.transpose(qkv_turn, (0, 2, 3, 1, 4)).reshape(D, 3, head_cols)
    embedded_sub = lax.all_to_all(
        embedded_sub.reshape(dp_size, sub_len, D), "dp", split_axis=0, concat_axis=0
    )
    embedded_sub = jnp.sum(embedded_sub.astype(f32), 0).astype(bf16)
    embedded = by_order(chip_bit, embedded_sub, xor_permute(embedded_sub, "blk", 2), 0)
    embedded, mid_all = together(embedded, mid_all)
    embedded = embedded.reshape(half_len, D).astype(f32)
    my_local, my_counted, _ = doc_layout(lengths[0], row_len)
    half_start = core_bit * half_len
    local_half = lax.dynamic_slice_in_dim(my_local, half_start, half_len, 0)
    pos_hit = (local_half[:, None] == jnp.arange(row_len, dtype=jnp.int32)[None, :]).astype(f32)
    stream = embedded + jnp.dot(pos_hit, positions, precision=HIGHEST)

    gain_one, shift_one, bias_q, bias_v, bias_o, gain_two, shift_two = (
        gains_biases[k] for k in range(7)
    )
    ff_rows = FF // D
    bias_fc = gains_biases[7 : 7 + ff_rows].reshape(FF)
    bias_proj = gains_biases[7 + ff_rows]
    gain_fin = gains_biases[8 + ff_rows]
    shift_fin = gains_biases[9 + ff_rows]

    def cut(vector, width):
        return lax.dynamic_slice_in_dim(vector, blk_index * width, width, 0)

    w_out = mid_all[:, rows_here:].reshape(dp_size, rows_here, col_part)
    w_out = jnp.transpose(w_out, (1, 0, 2)).reshape(head_cols, D)
    w_up = jnp.transpose(turn(mid_all[:, :rows_here]), (0, 2, 1, 3)).reshape(D, ff_part)
    w_down = down_all.reshape(dp_size, ff_part, col_part)
    w_down = jnp.transpose(w_down, (1, 0, 2)).reshape(ff_part, D)

    def turn_pair(value, axis, bit):
        return jnp.where(bit == 0, value, jnp.flip(value, axis))

    def own_order(value):
        value = value.reshape(dp_size, 2, half_len).transpose(1, 0, 2)
        return turn_pair(value, 0, core_bit).reshape(-1)

    own_ids = own_order(every_ids)
    own_targets = own_order(every_targets)
    own_counted = own_order(every_counted)
    own_local = own_order(every_local)

    token_blocks = total_rows // 128
    block_targets = own_targets.reshape(token_blocks, 128)
    block_counted = own_counted.astype(f32).reshape(token_blocks, 128)

    normed = join_half(layer_norm(stream, gain_one, shift_one).astype(bf16), core_bit)
    bias_q_cut, bias_v_cut = cut(bias_q, head_cols), cut(bias_v, head_cols)
    qkv_bias = jnp.stack([bias_q_cut, jnp.zeros_like(bias_q_cut), bias_v_cut])
    qkv_low = (dot("sd,dke->ske", normed, w_qkv) + qkv_bias).astype(bf16)
    heads_here = head_cols // HDIM
    split = qkv_low.reshape(row_len, 3, heads_here, HDIM)
    score_scale = 1.0 / math.sqrt(HDIM)
    scores = dot("shd,thd->hst", split[:, 0], split[:, 1]) * score_scale
    probs = jax.nn.softmax(jnp.where(attn_mask[None], scores, -1e30), axis=-1)
    probs_low = probs.astype(bf16)
    mixed = dot("hst,thd->shd", probs_low, split[:, 2]).astype(bf16).reshape(row_len, head_cols)
    last = blk_index == blk_size - 1
    mixed_row = jnp.concatenate(
        [xor_permute(mixed, "blk", k) for k in range(blk_size - 1, 0, -1)] + [mixed], 1
    )
    in_row = jnp.where(last, mixed_row, normed)
    mixed_sum = sum_half(jnp.dot(mixed, w_out, preferred_element_type=f32), core_bit)
    mixed_sum, block_targets, block_counted, own_ids, own_local, total_count = together(
        mixed_sum, block_targets, block_counted, own_ids, own_local, total_count
    )
    middle = stream + mixed_sum + bias_o

    normed_two_half = layer_norm(middle, gain_two, shift_two).astype(bf16)
    normed_two = join_half(normed_two_half, core_bit)
    slim_in = lax.all_gather(normed_two, "dp", axis=0).reshape(-1, D)
    hidden = jnp.dot(normed_two, w_up, preferred_element_type=f32) + cut(bias_fc, ff_part)
    active = jax.nn.gelu(hidden, approximate=True).astype(bf16)
    stream_out = (
        middle
        + sum_half(jnp.dot(active, w_down, preferred_element_type=f32), core_bit)
        + bias_proj
    )
    final_half = layer_norm(stream_out, gain_fin, shift_fin).astype(bf16)

    up_far = xor_permute(w_up, "blk", 2)
    down_far = xor_permute(w_down, "blk", 2)
    bias_group = jnp.stack(
        [
            lax.dynamic_slice_in_dim(bias_fc, (blk_index ^ k) * ff_part, ff_part, 0)
            for k in (0, 2, 1, 3)
        ]
    )

    in_side = lax.all_gather(in_row, "dp", axis=0).reshape(-1, D)
    in_scale = 1.0 / tokens
    out_scale = total_count * total_count / tokens
    share = max(256, FF // (2 * dp_size))
    spot = jnp.stack([chip_bit, dp_index % (FF // (2 * share)) * share])

    final_own, final_far = gather_half(final_half)
    final_own, up_far = together(final_own, up_far)
    table_rows = 128 * -(-piece_rows // 128)
    table_pad = jnp.pad(table_low, ((0, table_rows - piece_rows), (0, 0)))
    base_row = row_base.reshape(1).astype(jnp.int32)
    logits, log_here, hit_sum = head_logits(
        base_row, block_targets, block_counted, table_pad, final_own, final_far, piece_rows
    )
    log_every = spread(log_here, ("dp", "blk"))
    log_every, down_far = together(log_every, down_far)
    sources = lax.broadcasted_iota(jnp.int32, (dp_size * blk_size, 1, 1), 0)
    log_every = jnp.where(
        sources % 2 == core_bit, log_every, jnp.roll(log_every, token_blocks // 2, 1)
    )
    log_top = jnp.max(log_every, 0)
    log_total = log_top + jnp.log(jnp.sum(jnp.exp(log_every - log_top[None]), 0))
    loss_rest = jnp.sum(block_counted * (log_total + zloss_weight * log_total * log_total))
    head_own, head_far, glog = head_back(
        base_row,
        block_targets,
        block_counted / total_count,
        log_total,
        table_pad,
        logits,
        piece_rows,
    )
    head_got = xor_permute(head_far, "blk", 1).reshape(dp_size, 2, sub_len, D)
    head_own = head_own.reshape(dp_size, 2, sub_len, D)

    def chip_part(bit):
        return lax.dynamic_index_in_dim(
            head_own, bit, 1, False
        ) + lax.dynamic_index_in_dim(head_got, bit, 1, False).astype(f32)

    head_sent = xor_permute(chip_part(1 - chip_bit).astype(bf16), "blk", 2)
    head_keep = chip_part(chip_bit) + head_sent.astype(f32)
    head_rows = lax.all_to_all(head_keep.astype(bf16), "dp", split_axis=0, concat_axis=0)

    ups = (w_up, up_far, xor_permute(w_up, "blk", 1), xor_permute(up_far, "blk", 1))
    downs = (w_down, down_far, xor_permute(w_down, "blk", 1), xor_permute(down_far, "blk", 1))
    wide = wide_start(spot, bias_group, slim_in, ups)
    head_rows, in_side, wide = together(head_rows, in_side, wide)
    inv_in = approx_inverse((in_side,), jnp.full((1,), in_scale, f32))
    head_sub = jnp.sum(head_rows.astype(f32), 0)
    grad_final = by_order(chip_bit, head_sub, xor_permute(head_sub, "blk", 2), 0)
    grad_final = grad_final.reshape(half_len, D)
    table_grad = jnp.dot(
        glog, jnp.concatenate([final_own, final_far], 0), preferred_element_type=f32
    )[:piece_rows]

    grad_out, d_gain_fin, d_shift_fin = norm_back(stream_out, gain_fin, grad_final)
    grad_proj_half = grad_out.astype(bf16)
    grad_proj = join_half(grad_proj_half, core_bit)
    slim_mine = spread(grad_proj_half, "dp")
    slim_out = by_order(core_bit, slim_mine, xor_permute(slim_mine, "blk", 1), 1).reshape(-1, D)
    col_start = (dp_index * col_part).reshape(1)
    grad_active = dot("sd,fd->sf", grad_proj, w_down)
    _, gelu_pull = jax.vjp(lambda value: jax.nn.gelu(value, approximate=True), hidden)
    grad_fc = gelu_pull(grad_active)[0].astype(bf16)
    back_two = sum_half(dot("sf,df->sd", grad_fc, w_up), core_bit)
    back_two, inv_in = together(back_two, inv_in)
    back_middle, d_gain_two, d_shift_two = norm_back(middle, gain_two, back_two)
    grad_middle = grad_out + back_middle
    grad_attn_half = grad_middle.astype(bf16)
    grad_attn = join_half(grad_attn_half, core_bit)
    grad_mixed = (
        dot("se,de->sd", grad_attn, w_out).astype(bf16).reshape(row_len, heads_here, HDIM)
    )
    grad_value = dot("hst,shd->thd", probs_low, grad_mixed)
    grad_probs = dot("shd,thd->hst", grad_mixed, split[:, 2])
    grad_scores = (
        probs * (grad_probs - jnp.sum(grad_probs * probs, -1, keepdims=True))
    ).astype(bf16)
    grad_query = dot("hst,thd->shd", grad_scores, split[:, 1]) * score_scale
    grad_key = dot("hst,shd->thd", grad_scores, split[:, 0]) * score_scale
    grad_qkv = (
        jnp.stack([grad_query, grad_key, grad_value], 1)
        .reshape(row_len, 3, head_cols)
        .astype(bf16)
    )
    back_one = sum_half(dot("ske,dke->sd", grad_qkv, w_qkv), core_bit)
    slim_scale = jnp.where(chip_bit == 0, out_scale, in_scale).reshape(1)
    slim = jnp.where(chip_bit == 0, slim_out, slim_in)
    inv_slim, start_slim = slim_inverse((slim,), slim_scale, col_start)
    back_one, inv_slim = together(back_one, inv_slim)
    back_stream, d_gain_one, d_shift_one = norm_back(stream, gain_one, back_one)
    grad_stream = grad_middle + back_stream
    grad_embed_half = grad_stream.astype(bf16)

    pair_blocks = jnp.stack([grad_qkv[:, 0], grad_qkv[:, 1], grad_qkv[:, 2], grad_qkv[:, 2]], 0)
    pair_got = lax.all_to_all(pair_blocks, "blk", split_axis=0, concat_axis=0)
    pair_got, table_grad = together(pair_got, table_grad)
    pair_row = jnp.transpose(pair_got, (1, 0, 2)).reshape(row_len, D)
    out_row = jnp.where(last, grad_attn, pair_row)
    out_side = lax.all_gather(out_row, "dp", axis=0).reshape(-1, D)

    wide, out_row, grad_embed_half = together(wide, out_row, grad_embed_half)
    wide, gram, tops_here = wide_back(spot, wide, slim_out, downs, share)
    wide_scale = jnp.where(chip_bit == 0, in_scale, out_scale)
    gram_top = tops_here[0]
    top_part = tops_here[1] * wide_scale
    out_side, gram = together(out_side, gram)
    lead = (chip_bit == 0).astype(f32)

    def column_sum(value):
        return jnp.sum(value.astype(f32), 0, keepdims=True)

    lanes = lax.broadcasted_iota(jnp.int32, (1, D), 1)

    def place(vector):
        return jnp.where(lanes // head_cols == blk_index, jnp.tile(vector, (1, blk_size)), 0.0)

    ff_place = lax.broadcasted_iota(jnp.int32, (ff_rows, 1), 0) // (ff_rows // blk_size)
    small_part = jnp.concatenate(
        [
            lead * d_gain_one,
            lead * d_shift_one,
            place(column_sum(grad_qkv[:, 0])),
            place(column_sum(grad_qkv[:, 2])),
            lead * column_sum(grad_attn_half),
            lead * d_gain_two,
            lead * d_shift_two,
            jnp.where(ff_place == blk_index, column_sum(grad_fc), 0.0),
            lead * column_sum(grad_proj_half),
            lead * d_gain_fin,
            lead * d_shift_fin,
        ],
        0,
    )
    small_count = small_part.shape[0]
    small_part = small_part + xor_permute(small_part, "blk", 1)
    small_part = small_part + xor_permute(small_part, "blk", 2)
    small_part, top_part = together(small_part, top_part)
    small_every = spread(
        jnp.concatenate([small_part, jnp.full((2, D), top_part, f32)], 0), "dp"
    )
    grad_small = jnp.sum(small_every[:, :small_count], 0)
    top_pair = jnp.max(small_every[:, small_count:, :128], (0, 1), keepdims=True)
    wide_top = jnp.maximum(top_pair, xor_permute(top_pair, "blk", 1))[0, 0, 0] + 1e-06

    pre_small, small_square = pair_factor(
        (in_side,), (out_side,), inv_in, out_scale.reshape(1), col_start, col_part
    )
    pre_attn = lax.all_to_all(
        pre_small.reshape(blk_size, head_cols, col_part), "blk", split_axis=0, concat_axis=0
    )
    pre_attn = jnp.transpose(pre_attn, (1, 0, 2))[None]
    start_slim = jnp.pad(start_slim[:, :col_part], ((0, 0), (0, wide_part - col_part)))
    col_block = dp_index * wide_part // ff_part
    place_at = blk_index ^ col_block
    place_at = (place_at % 2) * 2 + place_at // 2
    start_wide = lax.dynamic_slice_in_dim(
        wide, place_at * ff_part + dp_index * wide_part % ff_part, wide_part, 1
    ).astype(f32)
    power = jnp.where(chip_bit == 0, start_slim, start_wide)
    ratio = gram_top * wide_scale / wide_top
    coef = series()
    coefs = jnp.stack(
        [coef[0] * jnp.ones_like(ratio), coef[1] * ratio, coef[2] * ratio**2, coef[3] * ratio**3]
    )
    left_own = lax.dynamic_slice_in_dim(inv_slim, blk_index * head_cols, head_cols, 0)
    left_far = lax.dynamic_slice_in_dim(inv_slim, (blk_index ^ 2) * head_cols, head_cols, 0)
    down_both, up_both, wide_square = wide_finish(
        chip_bit.reshape(1),
        coefs,
        gram,
        power,
        wide,
        slim_in,
        jnp.concatenate([left_own, left_far], 0),
        col_part,
    )
    low_chips = [k for k in range(blk_size) if k < 2]
    pre_proj = jnp.where(
        chip_bit == 0,
        down_both[0],
        lax.ppermute(down_both[1], "blk", [(k, k ^ 2) for k in low_chips]),
    ).T[None]
    pre_fc = jnp.where(
        chip_bit == 0,
        lax.ppermute(up_both[head_cols:], "blk", [(k ^ 2, k) for k in low_chips]),
        up_both[:head_cols],
    )[None]
    squares = small_square[0] + wide_square[0]

    grad_embed = jnp.concatenate(gather_half(grad_embed_half), 0)
    id_hit = (vocab_slots[:, None] == own_ids[None, :]).astype(bf16)
    table_grad = table_grad + jnp.dot(id_hit, grad_embed, preferred_element_type=f32)
    pos_all = (
        jnp.arange(row_len, dtype=jnp.int32)[:, None] == own_local[None, :]
    ).astype(bf16)
    grad_pos = jnp.dot(pos_all, grad_embed, preferred_element_type=f32)

    squares = squares + jnp.sum(table_grad * table_grad)
    lane = lax.broadcasted_iota(jnp.int32, (8, 128), 1)
    every_squares = spread(jnp.where(lane == 0, squares, hit_sum[0]), ("dp", "blk"))[:, 0, :2]
    every_squares = jnp.sum(every_squares, 0)
    loss_sum = loss_rest - every_squares[1]
    all_squares = (
        every_squares[0] + jnp.sum(grad_small * grad_small) + jnp.sum(grad_pos * grad_pos)
    )
    grad_norm = jnp.sqrt(all_squares)
    clip_factor = clip_level / jnp.maximum(grad_norm, clip_level)
    emb_out = adam_update(embedding, emb_mean, emb_var, table_grad, clip_factor, weight_decay)
    pos_out = adam_update(positions, pos_mean, pos_var, grad_pos, clip_factor, weight_decay)
    gains_out = adam_update(gains_biases, gains_mean, gains_var, grad_small, clip_factor, 0.0)
    attn_out = adam_update(w_attn, attn_mean, attn_var, pre_attn, clip_factor, weight_decay)
    fc_out = adam_update(w_fc, fc_mean, fc_var, pre_fc, clip_factor, weight_decay)
    proj_out = adam_update(w_proj, proj_mean, proj_var, pre_proj, clip_factor, weight_decay)
    return (
        (loss_sum, total_count, grad_norm)
        + emb_out
        + pos_out
        + gains_out
        + attn_out
        + fc_out
        + proj_out
    )


def solution(mesh):
    token = P("dp", None)
    table = P(("dp", "blk"), None)
    attn = P(None, "blk", None, "dp")
    flat = P(None, "blk", "dp")
    return jax.shard_map(
        body,
        mesh=mesh,
        in_specs=(token,) * 2
        + (table,) * 3
        + (P(),) * 6
        + (attn,) * 3
        + (flat,) * 6,
        out_specs=(P(),) * 3 + (table,) * 3 + (P(),) * 6 + (attn,) * 3 + (flat,) * 6,
        check_vma=False,
    )
```

time: 663 us -> 535 us (0.81)
  blocking collectives: 132 us -> 0 us
  Pallas kernels: 0 us -> 88.1 us
  matrix products: 118 us -> 32.3 us
  starting transfers between devices: 93.3 us -> 138 us
  waiting for transfers between devices: 153 us -> 112 us
    all_gather x3 -> x0, blocking collectives: 98.5 us -> none  [the longest x1 44.9 us: body(): slim_mine = lax.all_gather(slim_rows, 'dp', axis=0).reshape(-1, D)]
    pallas_call x0 -> x8, Pallas kernels: none -> 88.1 us  [the longest x1 20.4 us: wide_back(): pl.pallas_call(functools.partial(wide_back_kernel, parts, 384, share), ou...]
    dot_general x19 -> x9, matrix products: 60 us -> 6.05 us  [dot(): return jnp.einsum(spec, left, right, preferred_element_type=f32)]
    all_gather x5, waiting for transfers between devices: 39.4 us -> 0.07 us  [the longest x1 0.02 us: body(): slim_in = lax.all_gather(normed_two, 'dp', axis=0).reshape(-1, D)]
    dot_general x13 -> x1, matrix products: 44 us -> 6.95 us  [body(): jnp.dot(glog, jnp.concatenate([final_own, final_far], 0), preferred_eleme...]
    all_to_all x2 -> x0, blocking collectives: 33.9 us -> none  [the longest x1 22 us: spread(): return lax.all_to_all(copies, axes, split_axis=0, concat_axis=0)]
    ppermute x28 -> x46, starting transfers between devices: 40.2 us -> 64.1 us  [xor_permute(): return lax.ppermute(value, axis, [(k, k ^ bit) for k in range(size)])]
    reshape x14 -> x16, local copies, waits for them, and re-layouts: 22.3 us -> 9.35 us  [the longest x1 3.84 us: body(): w_down = down_all.reshape(dp_size, ff_part, col_part)]
  transfers between devices with their start and end apart: 44 -> 64, of which waited for: 25 -> 20; matrix products, arithmetic and copies ran while one was open for 22% -> 23% of each run, Pallas kernels for 0% -> 17%
where the time goes in v2:
time: 535 us; the launch traced here: 527 us
  starting transfers between devices  138 us (26%)
  waiting for transfers between devices  112 us (21%)
  Pallas kernels  88.1 us (16%)
  local copies, waits for them, and re-layouts  68.7 us (13%)
  other arithmetic  61.4 us (11%)
  matrix products  32.3 us (6%)
  between operations  26.8 us (5%)
    ppermute x46, waiting for transfers between devices, xor_permute(): return lax.ppermute(value, axis, [(k, k ^ bit) for k in range(size)])  72.1 us
    ppermute x46, starting transfers between devices, xor_permute(): return lax.ppermute(value, axis, [(k, k ^ bit) for k in range(size)])  64.1 us
    all_to_all x7, starting transfers between devices, spread(): return lax.all_to_all(copies, axes, split_axis=0, concat_axis=0)  37.6 us
    all_to_all x7, waiting for transfers between devices, spread(): return lax.all_to_all(copies, axes, split_axis=0, concat_axis=0)  35.6 us
    unnamed x230, local copies, waits for them, and re-layouts  22.6 us
    pallas_call x1, Pallas kernels, wide_back(): pl.pallas_call(functools.partial(wide_back_kernel, parts, 384, share), ou...  20.4 us
    sub x6, other arithmetic, adam_update(): weights - learn_rate * (mean_hat / (jnp.sqrt(var_hat) + adam_eps) + decay...  17.9 us
    all_to_all x1, starting transfers between devices, body(): lax.all_to_all(embedded_sub.reshape(dp_size, sub_len, D), 'dp', split_axi...  16.1 us
  transfers between devices with their start and end apart: 64, of which 20 were waited for; matrix products, arithmetic and copies ran while one was open for 23% of the time, Pallas kernels for 17%

profile of v2, /device:TPU:1, one launch (start us, length us, event | category | flops | bytes accessed | tf_op | source)
XLA Modules:
  0.0 527.1 jit_solution(5650846414648765765)
XLA Ops:
  13.8 2.4 collective-permute-start.3
  18.3 4.7 all-to-all-start
  25.1 2.6 convert_element_type.164
  30.6 3.2 collective-permute-start.5
  35.1 14.6 %collective-permute-done.5 = s32[144]{0:T(256)S(1)} collective-permute-done((s32[144]{0:T(256)S(1)}, s32[144]{0:T(256)S(1)}, u32[]{:S(2)}, u32[]{:S(2)}) %collective-permute-start.5) | collective-permute-done | bytes 608 | tf_op jit(solution)/shard_map/ppermute | solution.py:38
  53.3 4.4 collective-permute-start.7
  63.8 9.5 %collective-permute-done.8 = bf16[256,768]{1,0:T(8,128)(2,1)S(1)} collective-permute-done((bf16[256,768]{1,0:T(8,128)(2,1)S(1)}, bf16[256,768]{1,0:T(8,128)(2,1)S(1)}, u32[]{:S(2)}, u32[]{:S(2)}) %collective-permute-start.8) | collective-permute-done | bytes 393248 | tf_op jit(solution)/shard_map/ppermute | solution.py:38
  74.2 16.1 %all-to-all-start.1 = ((bf16[8,32,768]{2,1,0:T(8,128)(2,1)}), bf16[8,32,768]{2,1,0:T(8,128)(2,1)S(1)}, u32[]{:S(2)}, u32[]{:S(2)}) async-start(bf16[8,32,768]{2,1,0:T(8,128)(2,1)} %bitcast.18), calls=%async_computation.1 | async-start | bytes 786432 | tf_op jit(solution)/shard_map/all_to_all | solution.py:821
  95.4 7.0 %collective-permute-done.12 = bf16[2,192,288]{1,2,0:T(8,128)(2,1)S(1)} collective-permute-done((bf16[2,192,288]{1,2,0:T(8,128)(2,1)S(1)}, bf16[2,192,288]{1,2,0:T(8,128)(2,1)S(1)}, u32[]{:S(2)}, u32[]{:S(2)}) %collective-permute-start.12) | collective-permute-done | bytes 221216 | tf_op jit(solution)/shard_map/ppermute | solution.py:38
  102.4 6.8 %collective-permute-done.13 = bf16[2,192,288]{1,2,0:T(8,128)(2,1)S(1)} collective-permute-done((bf16[2,192,288]{1,2,0:T(8,128)(2,1)S(1)}, bf16[2,192,288]{1,2,0:T(8,128)(2,1)S(1)}, u32[]{:S(2)}, u32[]{:S(2)}) %collective-permute-start.13) | collective-permute-done | bytes 221216 | tf_op jit(solution)/shard_map/ppermute | solution.py:38
  129.6 3.8 reshape.745
  136.5 2.4 fusion.85
  146.9 2.5 multiply_convert_fusion
  152.7 5.1 collective-permute-done.21
  159.3 5.6 %all-to-all-start.2 = ((bf16[8,64,768]{2,1,0:T(8,128)(2,1)}), bf16[8,64,768]{2,1,0:T(8,128)(2,1)S(1)}, u32[]{:S(2)}, u32[]{:S(2)}) async-start(bf16[8,64,768]{2,1,0:T(8,128)(2,1)} %broadcast_in_dim.97), calls=%async_computation.2 | async-start | bytes 1572864 | tf_op jit(solution)/shard_map/all_to_all | solution.py:46
  167.8 21.1 %all-to-all-done.2 = bf16[8,64,768]{2,1,0:T(8,128)(2,1)S(1)} async-done(((bf16[8,64,768]{2,1,0:T(8,128)(2,1)}), bf16[8,64,768]{2,1,0:T(8,128)(2,1)S(1)}, u32[]{:S(2)}, u32[]{:S(2)}) %all-to-all-start.2) | async-done | bytes 786464 | tf_op jit(solution)/shard_map/all_to_all | solution.py:46
  195.3 8.1 %shard_map.355 = (f32[1664,1024]{1,0:T(8,128)S(1)}, f32[8,128]{1,0:T(8,128)S(1)}, f32[1]{0:T(128)}) custom-call(s32[1]{0:T(128)} %bitcast.51.base_ref, s32[8,128]{1,0:T(8,128)S(1)} %reshape_reshape.3.target_ref, f32[8,128]{1,0:T(8,128)S(1)} %reshape.768.counted_ref, bf16[1664,768]{1,0:T(8,128)(2,1)S(1)} %pad.11.table_ref, bf16[512,768]{1,0:T(8,128)(2,1)S(1)} %bitcast.419, ...), custom_call_target="tpu_custom_call" | custom-call | flops 1048576 | bytes 65536 | tf_op jit(solution)/shard_map/pallas_call | solution.py:395
  203.5 2.7 copy-done.3
  206.9 5.9 %all-to-all-start.3 = ((f32[32,8,128]{2,1,0:T(8,128)}), f32[32,8,128]{2,1,0:T(8,128)}, u32[]{:S(2)}, u32[]{:S(2)}) async-start(f32[32,8,128]{2,1,0:T(8,128)} %broadcast_in_dim.98), calls=%async_computation.3 | async-start | bytes 262144 | tf_op jit(solution)/shard_map/all_to_all | solution.py:46
  215.1 5.9 %collective-permute-done.27 = bf16[128,192]{0,1:T(8,128)(2,1)} collective-permute-done((bf16[128,192]{0,1:T(8,128)(2,1)}, bf16[128,192]{0,1:T(8,128)(2,1)}, u32[]{:S(2)}, u32[]{:S(2)}) %collective-permute-start.27) | collective-permute-done | bytes 49184 | tf_op jit(solution)/shard_map/ppermute | solution.py:38
  228.8 8.9 %shard_map.356 = (f32[512,768]{1,0:T(8,128)S(1)}, bf16[512,768]{1,0:T(8,128)(2,1)}, bf16[1664,1024]{1,0:T(8,128)(2,1)}) custom-call(s32[1]{0:T(128)} %bitcast.51.base_ref, s32[8,128]{1,0:T(8,128)S(1)} %reshape_reshape.3.target_ref, f32[8,128]{1,0:T(8,128)S(1)} %get-tuple-element.318.weight_ref, f32[8,128]{1,0:T(8,128)S(1)} %get-tuple-element.268.log_ref, ...), custom_call_target="tpu_custom_call" | custom-call | flops 1048576 | bytes 65536 | tf_op jit(solution)/shard_map/pallas_call | solution.py:453
  246.1 8.8 %collective-permute-done.26 = bf16[8,32,768]{2,1,0:T(8,128)(2,1)} collective-permute-done((bf16[8,32,768]{2,1,0:T(8,128)(2,1)}, bf16[8,32,768]{2,1,0:T(8,128)(2,1)}, u32[]{:S(2)}, u32[]{:S(2)}) %collective-permute-start.26) | collective-permute-done | bytes 393248 | tf_op jit(solution)/shard_map/ppermute | solution.py:38
  256.7 5.4 %all-to-all-start.4 = ((bf16[8,32,768]{2,1,0:T(8,128)(2,1)}), bf16[8,32,768]{2,1,0:T(8,128)(2,1)S(1)}, u32[]{:S(2)}, u32[]{:S(2)}) async-start(bf16[8,32,768]{2,1,0:T(8,128)(2,1)} %fusion.63), calls=%async_computation.4 | async-start | bytes 786432 | tf_op jit(solution)/shard_map/all_to_all | solution.py:953
  262.5 15.2 %shard_map.357.start_ref = bf16[1024,3072]{1,0:T(8,128)(2,1)} custom-call(s32[2]{0:T(128)S(1)} %pad_add_fusion.1.spot_ref, f32[4,768]{1,0:T(4,128)S(1)} %pad_maximum_fusion.16.bias_ref, bf16[1024,768]{1,0:T(8,128)(2,1)} %bitcast.414, bf16[768,768]{1,0:T(8,128)(2,1)} %bitcast.175.refs_0_, bf16[768,768]{1,0:T(8,128)(2,1)} %collective-permute-done.22.refs_1_, ...), custom_call_target="tpu_custom_call" | custom-call | flops 1048576 | bytes 65536 | tf_op jit(solution)/shard_map/pallas_call | solution.py:270
  278.1 3.4 collective-permute-start.32
  288.3 3.1 fusion.173
  305.1 6.9 %fusion.7 = f32[1572,768]{1,0:T(8,128)} fusion(bf16[1664,1024]{1,0:T(8,128)(2,1)} %get-tuple-element.85, bf16[512,768]{1,0:T(8,128)(2,1)S(1)} %copy-done.11, bf16[512,768]{1,0:T(8,128)(2,1)S(1)} %bitcast.420), kind=kOutput, calls=%fused_computation.8 | convolution fusion | flops 2475687936 | bytes 9629696 | tf_op jit(solution)/shard_map/dot_general | solution.py:963
  312.0 6.2 %shard_map.358.left_ref = f32[768,768]{1,0:T(8,128)S(1)} custom-call(f32[1]{0:T(128)} %constant.369.clone.1.scale_ref, bf16[1024,768]{1,0:T(8,128)(2,1)S(1)} %bitcast.416), custom_call_target="tpu_custom_call" | custom-call | flops 1048576 | bytes 65536 | tf_op jit(solution)/shard_map/pallas_call | solution.py:570
  320.6 5.8 %all-to-all-start.6 = ((bf16[8,64,768]{2,1,0:T(8,128)(2,1)}), bf16[8,64,768]{2,1,0:T(8,128)(2,1)S(1)}, u32[]{:S(2)}, u32[]{:S(2)}) async-start(bf16[8,64,768]{2,1,0:T(8,128)(2,1)} %broadcast_in_dim.100), calls=%async_computation.6 | async-start | bytes 1572864 | tf_op jit(solution)/shard_map/all_to_all | solution.py:46
  334.2 11.2 %all-to-all-done.6 = bf16[8,64,768]{2,1,0:T(8,128)(2,1)S(1)} async-done(((bf16[8,64,768]{2,1,0:T(8,128)(2,1)}), bf16[8,64,768]{2,1,0:T(8,128)(2,1)S(1)}, u32[]{:S(2)}, u32[]{:S(2)}) %all-to-all-start.6) | async-done | bytes 786464 | tf_op jit(solution)/shard_map/all_to_all | solution.py:46
  348.3 3.4 all-to-all-start.5
  351.9 4.2 all-to-all-done.5
  357.4 4.3 collective-permute-done.38
  364.4 7.8 %shard_map.359 = (f32[768,768]{1,0:T(8,128)S(1)}, f32[1024,128]{1,0:T(8,128)S(1)}) custom-call(f32[1]{0:T(128)} %bitcast.122.scale_ref, s32[1]{0:T(128)} %bitcast.73.first_ref, bf16[1024,768]{1,0:T(8,128)(2,1)S(1)} %broadcast_select_fusion.refs_0_), custom_call_target="tpu_custom_call" | custom-call | flops 1048576 | bytes 65536 | tf_op jit(solution)/shard_map/pallas_call | solution.py:585
  375.8 4.2 all-to-all-start.8
  382.7 20.4 %shard_map.360 = (bf16[1024,3072]{1,0:T(8,128)(2,1)}, bf16[1024,1024]{1,0:T(8,128)(2,1)}, f32[2]{0:T(128)}) custom-call(s32[2]{0:T(128)} %copy-done.18, bf16[1024,3072]{1,0:T(8,128)(2,1)} %shard_map.357.start_ref, bf16[1024,768]{1,0:T(8,128)(2,1)} %bitcast.425, bf16[768,768]{1,0:T(8,128)(2,1)} %copy.310.refs_0_, ...), custom_call_target="tpu_custom_call" | custom-call | flops 1048576 | bytes 65536 | tf_op jit(solution)/shard_map/pallas_call | solution.py:322
  403.1 8.7 %collective-permute-start.43 = (f32[14,768]{1,0:T(8,128)S(1)}, f32[14,768]{1,0:T(8,128)S(1)}, u32[]{:S(2)}, u32[]{:S(2)}) collective-permute-start(f32[14,768]{1,0:T(8,128)S(1)} %add.577), channel_id=1, source_target_pairs={{0,2},{1,3},{2,0},{3,1},{4,6},{5,7},{6,4},{7,5},{8,10},{9,11},{10,... | collective-permute-start | bytes 129032 | tf_op jit(solution)/shard_map/ppermute | solution.py:38
  414.7 6.1 %all-to-all-start.7 = ((f32[8,16,768]{2,1,0:T(8,128)}), f32[8,16,768]{2,1,0:T(8,128)S(1)}, u32[]{:S(2)}, u32[]{:S(2)}) async-start(f32[8,16,768]{2,1,0:T(8,128)} %broadcast_in_dim.105), calls=%async_computation.7 | async-start | bytes 786432 | tf_op jit(solution)/shard_map/all_to_all | solution.py:46
  426.7 3.2 all-to-all-done.7
  430.0 3.5 collective-permute-start.44
  439.4 12.6 %shard_map.361 = (f32[768,96]{1,0:T(8,128)}, f32[1]{0:T(128)}) custom-call(f32[1]{0:T(128)} %bitcast.72.scale_ref, s32[1]{0:T(128)} %bitcast.73.first_ref, f32[768,768]{1,0:T(8,128)S(1)} %copy-done.2, bf16[1024,768]{1,0:T(8,128)(2,1)S(1)} %bitcast.417, bf16[1024,768]{1,0:T(8,128)(2,1)S(1)} %bitcast.423), custom_call_target="tpu_custom_call" | custom-call | flops 1048576 | bytes 65536 | tf_op jit(solution)/shard_map/pallas_call | solution.py:603
  452.0 8.9 %shard_map.362 = (f32[2,96,768]{2,1,0:T(8,128)S(1)}, f32[384,384]{1,0:T(8,128)S(1)}, f32[1]{0:T(128)}) custom-call(s32[1]{0:T(128)} %bitcast.86.chip_ref, f32[4]{0:T(128)S(1)} %pad_maximum_fusion.18.coef_ref, bf16[1024,1024]{1,0:T(8,128)(2,1)} %get-tuple-element.98.gram_ref, f32[1024,384]{1,0:T(8,128)S(1)} %convert_select_fusion.start_ref, ...), custom_call_target="tpu_custom_call" | custom-call | flops 1048576 | bytes 65536 | tf_op jit(solution)/shard_map/pallas_call | solution.py:674
  462.4 7.5 %multiply_reduce_fusion = (f32[]{:T(128)}, f32[1572,768]{1,0:T(8,128)}) fusion(f32[1572,768]{1,0:T(8,128)S(1)} %bitcast.493, bf16[512,768]{1,0:T(8,128)(2,1)} %collective-permute-done.45, bf16[512,768]{1,0:T(8,128)(2,1)} %bitcast.137, s32[1024]{0:T(1024)S(1)} %copy-done.104, s32[1572]{0:T(1024)S(1)} %copy-done.95), kind=kOutput, calls=%fused_computation.6 | convolution fusion | flops 2480919552 | bytes 11241620 | tf_op jit(solution)/shard_map/dot_general | solution.py:1104
  471.9 5.3 %all-to-all-start.9 = ((f32[32,8,128]{2,1,0:T(8,128)}), f32[32,8,128]{2,1,0:T(8,128)S(1)}, u32[]{:S(2)}, u32[]{:S(2)}) async-start(f32[32,8,128]{2,1,0:T(8,128)} %broadcast_in_dim.117), calls=%async_computation.9 | async-start | bytes 262144 | tf_op jit(solution)/shard_map/all_to_all | solution.py:46
  478.2 4.0 collective-permute-start.47
  484.5 2.4 multiply_reduce_fusion.1
  486.9 5.3 %all-to-all-start.10 = ((f32[4,192,96]{2,1,0:T(8,128)}), f32[4,192,96]{2,1,0:T(8,128)S(1)}, u32[]{:S(2)}, u32[]{:S(2)}) async-start(f32[4,192,96]{2,1,0:T(8,128)} %bitcast.141), calls=%async_computation.10 | async-start | bytes 786432 | tf_op jit(solution)/shard_map/all_to_all | solution.py:1060
  494.9 12.9 %multiply_subtract_fusion = (f32[1572,768]{1,0:T(8,128)}, f32[1572,768]{1,0:T(8,128)}, f32[1572,768]{1,0:T(8,128)}) fusion(f32[1572,768]{1,0:T(8,128)} %param.22, f32[1572,768]{1,0:T(8,128)} %param.23, f32[1572,768]{1,0:T(8,128)} %param.24, f32[1572,768]{1,0:T(8,128)} %get-tuple-element.332, f32[]{:T(128)S(6)} %div.278), kind=kLoop, calls=%fused_computation.5 | loop fusion | flops 19316736 | bytes 33804292 | tf_op jit(solution)/shard_map/sub | solution.py:121
  (575 shorter events, 166.2 us)
Async XLA Ops:
  7.2 106.8 %all-gather.15.cloned.1.call-start = ((), (), s32[]{:S(2)}) async-start(), calls=%async_computation.15 | async-start | bytes 1658880 | tf_op jit(solution)/shard_map/all_gather | solution.py:781
  10.4 20.3 %collective-permute-start = (s32[144]{0:T(256)S(1)}, s32[144]{0:T(256)S(1)}, u32[]{:S(2)}, u32[]{:S(2)}) collective-permute-start(s32[144]{0:T(256)S(1)} %pad_add_fusion), channel_id=1, source_target_pairs={{0,4},{4,0},{8,12},{12,8},{16,20},{20,16},{24,28},{28,24},{1,5},{5... | collective-permute-start | bytes 1736 | tf_op jit(solution)/shard_map/ppermute | solution.py:38
  12.5 21.3 %collective-permute-start.1 = (s32[144]{0:T(256)S(1)}, s32[144]{0:T(256)S(1)}, u32[]{:S(2)}, u32[]{:S(2)}) collective-permute-start(s32[144]{0:T(256)S(1)} %pad_add_fusion), channel_id=1, source_target_pairs={{0,8},{4,12},{8,0},{12,4},{16,24},{20,28},{24,16},{28,20},{1,9},{5... | collective-permute-start | bytes 1736 | tf_op jit(solution)/shard_map/ppermute | solution.py:38
  13.8 21.3 %collective-permute-start.2 = (s32[144]{0:T(256)S(1)}, s32[144]{0:T(256)S(1)}, u32[]{:S(2)}, u32[]{:S(2)}) collective-permute-start(s32[144]{0:T(256)S(1)} %pad_add_fusion), channel_id=1, source_target_pairs={{0,12},{4,8},{8,4},{12,0},{16,28},{20,24},{24,20},{28,16},{1,13},{... | collective-permute-start | bytes 1736 | tf_op jit(solution)/shard_map/ppermute | solution.py:38
  13.8 21.3 %collective-permute-start.3 = (s32[144]{0:T(256)S(1)}, s32[144]{0:T(256)S(1)}, u32[]{:S(2)}, u32[]{:S(2)}) collective-permute-start(s32[144]{0:T(256)S(1)} %pad_add_fusion), channel_id=1, source_target_pairs={{0,16},{4,20},{8,24},{12,28},{16,0},{20,4},{24,8},{28,12},{1,17},{... | collective-permute-start | bytes 1736 | tf_op jit(solution)/shard_map/ppermute | solution.py:38
  16.2 18.8 %collective-permute-start.4 = (s32[144]{0:T(256)S(1)}, s32[144]{0:T(256)S(1)}, u32[]{:S(2)}, u32[]{:S(2)}) collective-permute-start(s32[144]{0:T(256)S(1)} %pad_add_fusion), channel_id=1, source_target_pairs={{0,20},{4,16},{8,28},{12,24},{16,4},{20,0},{24,12},{28,8},{1,21},{... | collective-permute-start | bytes 1736 | tf_op jit(solution)/shard_map/ppermute | solution.py:38
  18.3 55.8 %all-to-all-start = ((bf16[8,192,288]{1,2,0:T(8,128)(2,1)}), bf16[8,192,288]{1,2,0:T(8,128)(2,1)}, u32[]{:S(2)}, u32[]{:S(2)}) async-start(bf16[8,192,288]{1,2,0:T(8,128)(2,1)} %broadcast_in_dim.88), calls=%async_computation | async-start | bytes 2359296 | tf_op jit(solution)/shard_map/all_to_all | solution.py:46
  23.1 106.5 %all-gather.7.cloned.1.call-start = ((), (), s32[]{:S(2)}) async-start(), calls=%async_computation.11 | async-start | bytes 1327104 | tf_op jit(solution)/shard_map/all_gather | solution.py:782
  30.6 19.1 %collective-permute-start.5 = (s32[144]{0:T(256)S(1)}, s32[144]{0:T(256)S(1)}, u32[]{:S(2)}, u32[]{:S(2)}) collective-permute-start(s32[144]{0:T(256)S(1)} %pad_add_fusion), channel_id=1, source_target_pairs={{0,24},{4,28},{8,16},{12,20},{16,8},{20,12},{24,0},{28,4},{1,25},{... | collective-permute-start | bytes 1736 | tf_op jit(solution)/shard_map/ppermute | solution.py:38
  33.8 17.0 %collective-permute-start.6 = (s32[144]{0:T(256)S(1)}, s32[144]{0:T(256)S(1)}, u32[]{:S(2)}, u32[]{:S(2)}) collective-permute-start(s32[144]{0:T(256)S(1)} %pad_add_fusion), channel_id=1, source_target_pairs={{0,28},{4,24},{8,20},{12,16},{16,12},{20,8},{24,4},{28,0},{1,29},{... | collective-permute-start | bytes 1736 | tf_op jit(solution)/shard_map/ppermute | solution.py:38
  53.3 7.9 %collective-permute-start.7 = (bf16[2,256,768]{2,1,0:T(8,128)(2,1)S(1)}, bf16[2,256,768]{2,1,0:T(8,128)(2,1)}, u32[]{:S(2)}, u32[]{:S(2)}) collective-permute-start(bf16[2,256,768]{2,1,0:T(8,128)(2,1)S(1)} %pad_maximum_fusion.6), channel_id=1, source_target_pairs={{0,1},{1,0},{2,3},{3,2},{4,5},{5,4},{6,7},{7,6},{8,9},{9,8},{10,11... | collective-permute-start | bytes 2359304 | tf_op jit(solution)/shard_map/ppermute | solution.py:38
  62.6 10.8 %collective-permute-start.8 = (bf16[256,768]{1,0:T(8,128)(2,1)S(1)}, bf16[256,768]{1,0:T(8,128)(2,1)S(1)}, u32[]{:S(2)}, u32[]{:S(2)}) collective-permute-start(bf16[256,768]{1,0:T(8,128)(2,1)S(1)} %slice_bitcast_fusion), channel_id=1, source_target_pairs={{0,2},{1,3},{2,0},{3,1},{4,6},{5,7},{6,4},{7,5},{8,10},{9,11},{10,... | collective-permute-start | bytes 1179656 | tf_op jit(solution)/shard_map/ppermute | solution.py:38
  74.2 36.1 %all-to-all-start.1 = ((bf16[8,32,768]{2,1,0:T(8,128)(2,1)}), bf16[8,32,768]{2,1,0:T(8,128)(2,1)S(1)}, u32[]{:S(2)}, u32[]{:S(2)}) async-start(bf16[8,32,768]{2,1,0:T(8,128)(2,1)} %bitcast.18), calls=%async_computation.1 | async-start | bytes 786432 | tf_op jit(solution)/shard_map/all_to_all | solution.py:821
  90.3 172.1 %all-gather.11.cloned.1.call-start = ((), (), s32[]{:S(2)}) async-start(), calls=%async_computation.13 | async-start | bytes 1769472 | tf_op jit(solution)/shard_map/all_gather | solution.py:892
  93.7 8.7 %collective-permute-start.12 = (bf16[2,192,288]{1,2,0:T(8,128)(2,1)S(1)}, bf16[2,192,288]{1,2,0:T(8,128)(2,1)S(1)}, u32[]{:S(2)}, u32[]{:S(2)}) collective-permute-start(bf16[2,192,288]{1,2,0:T(8,128)(2,1)S(1)} %get-tuple-element.293), channel_id=1, source_target_pairs={{0,2},{1,3},{2,0},{3,1},{4,6},{5,7},{6,4},{7,5},{8,10},{9,11},{10,... | collective-permute-start | bytes 663560 | tf_op jit(solution)/shard_map/ppermute | solution.py:38
  94.9 14.2 %collective-permute-start.13 = (bf16[2,192,288]{1,2,0:T(8,128)(2,1)S(1)}, bf16[2,192,288]{1,2,0:T(8,128)(2,1)S(1)}, u32[]{:S(2)}, u32[]{:S(2)}) collective-permute-start(bf16[2,192,288]{1,2,0:T(8,128)(2,1)S(1)} %get-tuple-element.292), channel_id=1, source_target_pairs={{0,3},{1,2},{2,1},{3,0},{4,7},{5,6},{6,5},{7,4},{8,11},{9,10},{10,... | collective-permute-start | bytes 663560 | tf_op jit(solution)/shard_map/ppermute | solution.py:38
  119.0 17.5 %collective-permute-start.17 = (bf16[2,192,384]{2,0,1:T(2,128)(2,1)}, bf16[2,192,384]{2,0,1:T(2,128)(2,1)}, u32[]{:S(2)}, u32[]{:S(2)}) collective-permute-start(bf16[2,192,384]{2,0,1:T(2,128)(2,1)} %bitcast.407), channel_id=1, source_target_pairs={{0,1},{1,0},{2,3},{3,2},{4,5},{5,4},{6,7},{7,6},{8,9},{9,8},{10,11... | collective-permute-start | bytes 884744 | tf_op jit(solution)/shard_map/ppermute | solution.py:38
  120.0 16.4 %collective-permute-start.18 = (bf16[2,192,384]{2,0,1:T(2,128)(2,1)}, bf16[2,192,384]{2,0,1:T(2,128)(2,1)}, u32[]{:S(2)}, u32[]{:S(2)}) collective-permute-start(bf16[2,192,384]{2,0,1:T(2,128)(2,1)} %bitcast.406), channel_id=1, source_target_pairs={{0,2},{1,3},{2,0},{3,1},{4,6},{5,7},{6,4},{7,5},{8,10},{9,11},{10,... | collective-permute-start | bytes 884744 | tf_op jit(solution)/shard_map/ppermute | solution.py:38
  122.3 14.2 %collective-permute-start.19 = (bf16[2,192,384]{2,0,1:T(2,128)(2,1)}, bf16[2,192,384]{2,0,1:T(2,128)(2,1)}, u32[]{:S(2)}, u32[]{:S(2)}) collective-permute-start(bf16[2,192,384]{2,0,1:T(2,128)(2,1)} %bitcast.405), channel_id=1, source_target_pairs={{0,3},{1,2},{2,1},{3,0},{4,7},{5,6},{6,5},{7,4},{8,11},{9,10},{10,... | collective-permute-start | bytes 884744 | tf_op jit(solution)/shard_map/ppermute | solution.py:38
  159.3 29.6 %all-to-all-start.2 = ((bf16[8,64,768]{2,1,0:T(8,128)(2,1)}), bf16[8,64,768]{2,1,0:T(8,128)(2,1)S(1)}, u32[]{:S(2)}, u32[]{:S(2)}) async-start(bf16[8,64,768]{2,1,0:T(8,128)(2,1)} %broadcast_in_dim.97), calls=%async_computation.2 | async-start | bytes 1572864 | tf_op jit(solution)/shard_map/all_to_all | solution.py:46
  164.9 29.6 %collective-permute-start.22 = (bf16[768,768]{1,0:T(8,128)(2,1)}, bf16[768,768]{1,0:T(8,128)(2,1)}, u32[]{:S(2)}, u32[]{:S(2)}) collective-permute-start(bf16[768,768]{1,0:T(8,128)(2,1)} %bitcast.175.refs_0_), channel_id=1, source_target_pairs={{0,2},{1,3},{2,0},{3,1},{4,6},{5,7},{6,4},{7,5},{8,10},{9,11},{10,... | collective-permute-start | bytes 3538952 | tf_op jit(solution)/shard_map/ppermute | solution.py:38
  167.5 56.9 %collective-permute-start.24 = (bf16[768,768]{1,0:T(8,128)(2,1)}, bf16[768,768]{1,0:T(8,128)(2,1)}, u32[]{:S(2)}, u32[]{:S(2)}) collective-permute-start(bf16[768,768]{1,0:T(8,128)(2,1)} %copy.310.refs_0_), channel_id=1, source_target_pairs={{0,2},{1,3},{2,0},{3,1},{4,6},{5,7},{6,4},{7,5},{8,10},{9,11},{10,... | collective-permute-start | bytes 3538952 | tf_op jit(solution)/shard_map/ppermute | solution.py:38
  193.0 28.0 %collective-permute-start.27 = (bf16[128,192]{0,1:T(8,128)(2,1)}, bf16[128,192]{0,1:T(8,128)(2,1)}, u32[]{:S(2)}, u32[]{:S(2)}) collective-permute-start(bf16[128,192]{0,1:T(8,128)(2,1)} %bitcast.78), channel_id=1, source_target_pairs={{0,3},{1,2},{2,1},{3,0},{4,7},{5,6},{6,5},{7,4},{8,11},{9,10},{10,... | collective-permute-start | bytes 147464 | tf_op jit(solution)/shard_map/ppermute | solution.py:38
  194.2 26.8 %collective-permute-start.28 = (bf16[128,192]{0,1:T(8,128)(2,1)}, bf16[128,192]{0,1:T(8,128)(2,1)}, u32[]{:S(2)}, u32[]{:S(2)}) collective-permute-start(bf16[128,192]{0,1:T(8,128)(2,1)} %bitcast.78), channel_id=1, source_target_pairs={{0,2},{1,3},{2,0},{3,1},{4,6},{5,7},{6,4},{7,5},{8,10},{9,11},{10,... | collective-permute-start | bytes 147464 | tf_op jit(solution)/shard_map/ppermute | solution.py:38
  194.4 26.5 %collective-permute-start.29 = (bf16[128,192]{0,1:T(8,128)(2,1)}, bf16[128,192]{0,1:T(8,128)(2,1)}, u32[]{:S(2)}, u32[]{:S(2)}) collective-permute-start(bf16[128,192]{0,1:T(8,128)(2,1)} %bitcast.78), channel_id=1, source_target_pairs={{0,1},{1,0},{2,3},{3,2},{4,5},{5,4},{6,7},{7,6},{8,9},{9,8},{10,11... | collective-permute-start | bytes 147464 | tf_op jit(solution)/shard_map/ppermute | solution.py:38
  206.9 17.6 %all-to-all-start.3 = ((f32[32,8,128]{2,1,0:T(8,128)}), f32[32,8,128]{2,1,0:T(8,128)}, u32[]{:S(2)}, u32[]{:S(2)}) async-start(f32[32,8,128]{2,1,0:T(8,128)} %broadcast_in_dim.98), calls=%async_computation.3 | async-start | bytes 262144 | tf_op jit(solution)/shard_map/all_to_all | solution.py:46
  212.8 65.0 %all-gather.9.cloned.1.call-start = ((), (), s32[]{:S(2)}) async-start(), calls=%async_computation.12 | async-start | bytes 1769472 | tf_op jit(solution)/shard_map/all_gather | solution.py:911
  244.1 10.7 %collective-permute-start.26 = (bf16[8,32,768]{2,1,0:T(8,128)(2,1)}, bf16[8,32,768]{2,1,0:T(8,128)(2,1)}, u32[]{:S(2)}, u32[]{:S(2)}) collective-permute-start(bf16[8,32,768]{2,1,0:T(8,128)(2,1)} %fusion.74), channel_id=1, source_target_pairs={{0,2},{1,3},{2,0},{3,1},{4,6},{5,7},{6,4},{7,5},{8,10},{9,11},{10,... | collective-permute-start | bytes 1179656 | tf_op jit(solution)/shard_map/ppermute | solution.py:38
  245.4 17.0 %collective-permute-start.30 = (bf16[768,768]{1,0:T(8,128)(2,1)}, bf16[768,768]{1,0:T(8,128)(2,1)}, u32[]{:S(2)}, u32[]{:S(2)}) collective-permute-start(bf16[768,768]{1,0:T(8,128)(2,1)} %bitcast.175.refs_0_), channel_id=1, source_target_pairs={{0,1},{1,0},{2,3},{3,2},{4,5},{5,4},{6,7},{7,6},{8,9},{9,8},{10,11... | collective-permute-start | bytes 3538952 | tf_op jit(solution)/shard_map/ppermute | solution.py:38
  246.1 16.4 %collective-permute-start.31 = (bf16[768,768]{1,0:T(8,128)(2,1)}, bf16[768,768]{1,0:T(8,128)(2,1)}, u32[]{:S(2)}, u32[]{:S(2)}) collective-permute-start(bf16[768,768]{1,0:T(8,128)(2,1)} %collective-permute-done.22.refs_1_), channel_id=1, source_target_pairs={{0,1},{1,0},{2,3},{3,2},{4,5},{5,4},{6,7},{7,6},{8,9},{9,8},{10,11... | collective-permute-start | bytes 3538952 | tf_op jit(solution)/shard_map/ppermute | solution.py:38
  256.7 21.3 %all-to-all-start.4 = ((bf16[8,32,768]{2,1,0:T(8,128)(2,1)}), bf16[8,32,768]{2,1,0:T(8,128)(2,1)S(1)}, u32[]{:S(2)}, u32[]{:S(2)}) async-start(bf16[8,32,768]{2,1,0:T(8,128)(2,1)} %fusion.63), calls=%async_computation.4 | async-start | bytes 786432 | tf_op jit(solution)/shard_map/all_to_all | solution.py:953
  300.0 82.7 %collective-permute-start.40 = (bf16[768,768]{1,0:T(8,128)(2,1)}, bf16[768,768]{1,0:T(8,128)(2,1)}, u32[]{:S(2)}, u32[]{:S(2)}) collective-permute-start(bf16[768,768]{1,0:T(8,128)(2,1)} %copy.310.refs_0_), channel_id=1, source_target_pairs={{0,1},{1,0},{2,3},{3,2},{4,5},{5,4},{6,7},{7,6},{8,9},{9,8},{10,11... | collective-permute-start | bytes 3538952 | tf_op jit(solution)/shard_map/ppermute | solution.py:38
  302.1 80.6 %collective-permute-start.41 = (bf16[768,768]{1,0:T(8,128)(2,1)}, bf16[768,768]{1,0:T(8,128)(2,1)}, u32[]{:S(2)}, u32[]{:S(2)}) collective-permute-start(bf16[768,768]{1,0:T(8,128)(2,1)} %collective-permute-done.24.refs_1_), channel_id=1, source_target_pairs={{0,1},{1,0},{2,3},{3,2},{4,5},{5,4},{6,7},{7,6},{8,9},{9,8},{10,11... | collective-permute-start | bytes 3538952 | tf_op jit(solution)/shard_map/ppermute | solution.py:38
  303.3 23.1 %collective-permute-start.35 = (f32[64,768]{1,0:T(8,128)S(1)}, f32[64,768]{1,0:T(8,128)}, u32[]{:S(2)}, u32[]{:S(2)}) collective-permute-start(f32[64,768]{1,0:T(8,128)S(1)} %bitcast_add_fusion.5), channel_id=1, source_target_pairs={{0,2},{1,3},{2,0},{3,1},{4,6},{5,7},{6,4},{7,5},{8,10},{9,11},{10,... | collective-permute-start | bytes 589832 | tf_op jit(solution)/shard_map/ppermute | solution.py:38
  320.6 24.9 %all-to-all-start.6 = ((bf16[8,64,768]{2,1,0:T(8,128)(2,1)}), bf16[8,64,768]{2,1,0:T(8,128)(2,1)S(1)}, u32[]{:S(2)}, u32[]{:S(2)}) async-start(bf16[8,64,768]{2,1,0:T(8,128)(2,1)} %broadcast_in_dim.100), calls=%async_computation.6 | async-start | bytes 1572864 | tf_op jit(solution)/shard_map/all_to_all | solution.py:46
  333.8 22.3 %collective-permute-start.37 = (f32[64,768]{1,0:T(8,128)S(1)}, f32[64,768]{1,0:T(8,128)S(1)}, u32[]{:S(2)}, u32[]{:S(2)}) collective-permute-start(f32[64,768]{1,0:T(8,128)S(1)} %dynamic-slice_bitcast_fusion.3), channel_id=1, source_target_pairs={{0,1},{1,0},{2,3},{3,2},{4,5},{5,4},{6,7},{7,6},{8,9},{9,8},{10,11... | collective-permute-start | bytes 589832 | tf_op jit(solution)/shard_map/ppermute | solution.py:38
  345.5 16.3 %collective-permute-start.39 = (bf16[8,64,768]{2,1,0:T(8,128)(2,1)S(1)}, bf16[8,64,768]{2,1,0:T(8,128)(2,1)S(1)}, u32[]{:S(2)}, u32[]{:S(2)}) collective-permute-start(bf16[8,64,768]{2,1,0:T(8,128)(2,1)S(1)} %all-to-all-done.6), channel_id=1, source_target_pairs={{0,1},{1,0},{2,3},{3,2},{4,5},{5,4},{6,7},{7,6},{8,9},{9,8},{10,11... | collective-permute-start | bytes 2359304 | tf_op jit(solution)/shard_map/ppermute | solution.py:38
  348.3 7.8 %all-to-all-start.5 = ((bf16[4,128,192]{1,2,0:T(8,128)(2,1)}), bf16[4,128,192]{1,2,0:T(8,128)(2,1)S(1)}, u32[]{:S(2)}, u32[]{:S(2)}) async-start(bf16[4,128,192]{1,2,0:T(8,128)(2,1)} %pad_maximum_fusion.12), calls=%async_computation.5 | async-start | bytes 393216 | tf_op jit(solution)/shard_map/all_to_all | solution.py:1007
  351.6 83.3 %all-gather.13.cloned.1.call-start = ((), (), s32[]{:S(2)}) async-start(), calls=%async_computation.14 | async-start | bytes 1769472 | tf_op jit(solution)/shard_map/all_gather | solution.py:1011
  375.8 38.2 %all-to-all-start.8 = ((bf16[8,64,768]{2,1,0:T(8,128)(2,1)}), bf16[8,64,768]{2,1,0:T(8,128)(2,1)}, u32[]{:S(2)}, u32[]{:S(2)}) async-start(bf16[8,64,768]{2,1,0:T(8,128)(2,1)} %broadcast_in_dim.114), calls=%async_computation.8 | async-start | bytes 1572864 | tf_op jit(solution)/shard_map/all_to_all | solution.py:46
  380.8 22.3 %collective-permute-start.42 = (f32[14,768]{1,0:T(8,128)S(1)}, f32[14,768]{1,0:T(8,128)S(1)}, u32[]{:S(2)}, u32[]{:S(2)}) collective-permute-start(f32[14,768]{1,0:T(8,128)S(1)} %concatenate.63), channel_id=1, source_target_pairs={{0,1},{1,0},{2,3},{3,2},{4,5},{5,4},{6,7},{7,6},{8,9},{9,8},{10,11... | collective-permute-start | bytes 129032 | tf_op jit(solution)/shard_map/ppermute | solution.py:38
  403.1 10.8 %collective-permute-start.43 = (f32[14,768]{1,0:T(8,128)S(1)}, f32[14,768]{1,0:T(8,128)S(1)}, u32[]{:S(2)}, u32[]{:S(2)}) collective-permute-start(f32[14,768]{1,0:T(8,128)S(1)} %add.577), channel_id=1, source_target_pairs={{0,2},{1,3},{2,0},{3,1},{4,6},{5,7},{6,4},{7,5},{8,10},{9,11},{10,... | collective-permute-start | bytes 129032 | tf_op jit(solution)/shard_map/ppermute | solution.py:38
  414.7 15.2 %all-to-all-start.7 = ((f32[8,16,768]{2,1,0:T(8,128)}), f32[8,16,768]{2,1,0:T(8,128)S(1)}, u32[]{:S(2)}, u32[]{:S(2)}) async-start(f32[8,16,768]{2,1,0:T(8,128)} %broadcast_in_dim.105), calls=%async_computation.7 | async-start | bytes 786432 | tf_op jit(solution)/shard_map/all_to_all | solution.py:46
  424.7 37.7 %collective-permute-start.45 = (bf16[512,768]{1,0:T(8,128)(2,1)}, bf16[512,768]{1,0:T(8,128)(2,1)}, u32[]{:S(2)}, u32[]{:S(2)}) collective-permute-start(bf16[512,768]{1,0:T(8,128)(2,1)} %bitcast.137), channel_id=1, source_target_pairs={{0,1},{1,0},{2,3},{3,2},{4,5},{5,4},{6,7},{7,6},{8,9},{9,8},{10,11... | collective-permute-start | bytes 2359304 | tf_op jit(solution)/shard_map/ppermute | solution.py:38
  471.9 15.0 %all-to-all-start.9 = ((f32[32,8,128]{2,1,0:T(8,128)}), f32[32,8,128]{2,1,0:T(8,128)S(1)}, u32[]{:S(2)}, u32[]{:S(2)}) async-start(f32[32,8,128]{2,1,0:T(8,128)} %broadcast_in_dim.117), calls=%async_computation.9 | async-start | bytes 262144 | tf_op jit(solution)/shard_map/all_to_all | solution.py:46
  478.2 30.0 %collective-permute-start.47 = (f32[96,768]{1,0:T(8,128)S(1)}, f32[96,768]{1,0:T(8,128)}, u32[]{:S(2)}, u32[]{:S(2)}) collective-permute-start(f32[96,768]{1,0:T(8,128)S(1)} %slice_bitcast_fusion.2), channel_id=1, source_target_pairs={{0,2},{1,3},{4,6},{5,7},{8,10},{9,11},{12,14},{13,15},{16,18},{17,... | collective-permute-start | bytes 884744 | tf_op jit(solution)/shard_map/ppermute | solution.py:1093
  483.2 33.0 %collective-permute-start.46 = (f32[192,384]{1,0:T(8,128)S(1)}, f32[192,384]{1,0:T(8,128)}, u32[]{:S(2)}, u32[]{:S(2)}) collective-permute-start(f32[192,384]{1,0:T(8,128)S(1)} %slice.172), channel_id=1, source_target_pairs={{2,0},{3,1},{6,4},{7,5},{10,8},{11,9},{14,12},{15,13},{18,16},{19,... | collective-permute-start | bytes 884744 | tf_op jit(solution)/shard_map/ppermute | solution.py:1097
  486.9 20.8 %all-to-all-start.10 = ((f32[4,192,96]{2,1,0:T(8,128)}), f32[4,192,96]{2,1,0:T(8,128)S(1)}, u32[]{:S(2)}, u32[]{:S(2)}) async-start(f32[4,192,96]{2,1,0:T(8,128)} %bitcast.141), calls=%async_computation.10 | async-start | bytes 786432 | tf_op jit(solution)/shard_map/all_to_all | solution.py:1060
  (128 other events, 1032.0 us)
Sparse Core Ops, SparseCore 0:
  10.8 58.0 all-gather.14
  71.7 40.5 all-gather.6
  152.9 50.3 all-gather.10
  224.6 49.8 all-gather.8
  357.5 55.1 all-gather.12
